TPU v7x, 256 devices: a whole 4x4x8 slice. The times are simulated.
256 devices in a mesh: cam: 8 (over z_lo, core), tile: 32 (over x, z_hi, y).
Axes of the slice: x: 4, y: 4, z: 8 (z_hi: 2, z_lo: 4; z = z_hi * 4 + z_lo), core: 2. Of those that a mesh axis runs over, the one named last changes fastest.
Arguments:
- queries: bfloat16 [8192, 256], P('tile'), as said below
- keys: bfloat16 [16384, 256], P(('cam', 'tile')), as said below
- values: bfloat16 [16384, 256], P(('cam', 'tile')), may hold values from -6 to 6
- grad_out: bfloat16 [8192, 256], P('tile'), may hold values from -6 to 6
- visible: int32 [64, 512], P('tile', 'cam'), may hold values from 0 to 1, as said below
- counts: int32 [512], P('cam'), may hold values from 2 to 32
Outputs:
- grad_queries: bfloat16 [8192, 256], P('tile')
- grad_keys: bfloat16 [16384, 256], P(('cam', 'tile'))
- grad_values: bfloat16 [16384, 256], P(('cam', 'tile'))
Inputs may be any that keep to these rules, and one draw needn't show every extreme that they name: Every tile has at least one visible block. `queries`: projected query features. `keys`: projected key features.
All inputs are finite; a program needn't handle non-finite values.
Results may differ from a plain program's by a relative error of at most 0.0052.
Values may be sent and summed in bfloat16 or wider, within the bound.
A program may use at most 128 MiB of HBM per device.

v0:
```python
import math

import jax
import jax.numpy as jnp
from jax import lax
from jax.sharding import PartitionSpec as P

H = 8


def shards(queries, keys, values, grad_out, visible, counts):
    row_count, width = queries.shape
    head_dim = width // H
    scale = 1.0 / math.sqrt(head_dim)
    key_all, value_all = (
        lax.all_gather(keys, "tile", axis=0, tiled=True),
        lax.all_gather(values, "tile", axis=0, tiled=True),
    )
    group = key_all.shape[0]
    block_count = counts.shape[0]
    block_keys = group // block_count
    slot_index = jnp.arange(group, dtype=jnp.int32) % block_keys
    key_valid = slot_index < jnp.repeat(counts, block_keys)
    tile_count = visible.shape[0]
    tile_rows = row_count // tile_count
    mask_tiles = (jnp.repeat(visible, block_keys, axis=1) == 1) & key_valid[None, :]
    per_step = 2
    step_count = tile_count // per_step
    step_rows = per_step * tile_rows
    query_blocks = queries.reshape(step_count, step_rows, H, head_dim)
    grad_blocks = grad_out.reshape(step_count, step_rows, H, head_dim)
    mask_blocks = mask_tiles.reshape(step_count, per_step, group)
    key_heads = key_all.reshape(group, H, head_dim)
    value_heads = value_all.reshape(group, H, head_dim)

    def scores_of(query_blk, key_mat):
        return (
            jnp.einsum("qhd,khd->hqk", query_blk, key_mat, preferred_element_type=jnp.float32)
            * scale
        )

    def row_mask(mask_blk):
        return jnp.repeat(mask_blk, tile_rows, axis=0)[None, :, :]

    def local_stats(inputs):
        query_blk, mask_blk = inputs
        scores = scores_of(query_blk, key_heads)
        allowed = row_mask(mask_blk)
        top = jnp.max(jnp.where(allowed, scores, -1e30), axis=-1)
        total = jnp.sum(jnp.where(allowed, jnp.exp(scores - top[..., None]), 0.0), axis=-1)
        return (top, total)

    local_top, local_total = lax.map(local_stats, (query_blocks, mask_blocks))
    global_top = lax.pmax(local_top, "cam")
    global_total = lax.psum(local_total * jnp.exp(local_top - global_top), "cam")
    lse_all = global_top + jnp.log(global_total)

    def probs_terms(query_blk, grad_blk, mask_blk, lse_blk, key_mat, value_mat):
        scores = scores_of(query_blk, key_mat)
        allowed = row_mask(mask_blk)
        probs = jnp.where(allowed, jnp.exp(scores - lse_blk[..., None]), 0.0)
        dprobs = jnp.einsum("qhd,khd->hqk", grad_blk, value_mat, preferred_element_type=jnp.float32)
        return (probs, dprobs)

    def local_delta(inputs):
        query_blk, grad_blk, mask_blk, lse_blk = inputs
        probs, dprobs = probs_terms(query_blk, grad_blk, mask_blk, lse_blk, key_heads, value_heads)
        return jnp.sum(probs * dprobs, axis=-1)

    delta_part = lax.map(local_delta, (query_blocks, grad_blocks, mask_blocks, lse_all))
    delta_all = lax.psum(delta_part, "cam")

    def rounded_terms(query_blk, grad_blk, mask_blk, lse_blk, delta_blk, key_mat, value_mat):
        probs, dprobs = probs_terms(query_blk, grad_blk, mask_blk, lse_blk, key_mat, value_mat)
        dscores = probs * (dprobs - delta_blk[..., None])
        return (probs.astype(jnp.bfloat16), dscores.astype(jnp.bfloat16))

    def query_grad_of(dscores_b):
        grad_q = (
            jnp.einsum("hqk,khd->qhd", dscores_b, key_heads, preferred_element_type=jnp.float32)
            * scale
        )
        return grad_q.reshape(step_rows, width)

    def grad_step(carry, inputs):
        query_blk, grad_blk, mask_blk, lse_blk, delta_blk = inputs
        probs_b, dscores_b = rounded_terms(
            query_blk, grad_blk, mask_blk, lse_blk, delta_blk, key_heads, value_heads
        )
        grad_k = (
            carry[0]
            + jnp.einsum("hqk,qhd->khd", dscores_b, query_blk, preferred_element_type=jnp.float32)
            * scale
        )
        grad_v = carry[1] + jnp.einsum(
            "hqk,qhd->khd", probs_b, grad_blk, preferred_element_type=jnp.float32
        )
        return ((grad_k, grad_v), query_grad_of(dscores_b))

    zero_kv = jnp.zeros((group, H, head_dim), jnp.float32)
    (grad_k, grad_v), query_parts = lax.scan(
        grad_step, (zero_kv, zero_kv), (query_blocks, grad_blocks, mask_blocks, lse_all, delta_all)
    )
    joined = jnp.concatenate((grad_k.reshape(group, width), grad_v.reshape(group, width)), axis=1)
    owned = lax.psum_scatter(joined, "tile", scatter_dimension=0, tiled=True)
    grad_queries = lax.psum(query_parts.reshape(row_count, width), "cam").astype(jnp.bfloat16)
    grad_keys = owned[:, :width].astype(jnp.bfloat16)
    grad_values = owned[:, width:].astype(jnp.bfloat16)
    return (grad_queries, grad_keys, grad_values)


def solution(mesh):
    in_specs = (
        P("tile", None),
        P(("cam", "tile"), None),
        P(("cam", "tile"), None),
        P("tile", None),
        P("tile", "cam"),
        P("cam"),
    )
    out_specs = (P("tile", None), P(("cam", "tile"), None), P(("cam", "tile"), None))
    return jax.shard_map(shards, mesh=mesh, in_specs=in_specs, out_specs=out_specs, check_vma=False)
```

profile of v0, /device:TPU:32, one launch (start us, length us, event | category | flops | bytes accessed | tf_op | source)
XLA Modules:
  0.0 469.4 jit_solution(15476085039806583543)
XLA Ops:
  7.2 0.7 all-gather.3.cloned.1.call-update
  7.9 0.7 all-gather.5.cloned.1.call-update
  8.7 0.7 broadcast_in_dim.83
  9.5 0.7 broadcast_compare_fusion
  10.3 0.1 eq.14
  10.4 1.0 copy.18
  11.4 1.0 copy.20
  12.4 81.8 %all-gather.3.cloned.1.call-done = bf16[2048,256]{1,0:T(8,128)(2,1)} async-done(((bf16[64,256]{1,0:T(8,128)(2,1)}), bf16[2048,256]{1,0:T(8,128)(2,1)}) %all-gather.3.cloned.1.call-update) | async-done | bytes 1048592 | tf_op jit(solution)/shard_map/all_gather | solution.py:16
  94.2 1.5 copy.19
  95.7 0.2 broadcast_in_dim.84
  95.9 3.3 select_reduce_fusion.1
  99.2 5.7 %copy-done = f32[8,256,2048]{2,1,0:T(8,128)} copy-done((f32[8,256,2048]{2,1,0:T(8,128)}, f32[8,256,2048]{2,1,0:T(8,128)S(1)}, u32[]{:S(2)}) %copy-start) | copy-done | bytes 16777240
  104.9 4.6 select_reduce_fusion
  109.5 11.9 %pmax.7 = f32[1,8,256]{2,1,0:T(8,128)S(1)} all-reduce(f32[1,8,256]{2,1,0:T(8,128)S(1)} %bitcast.44), channel_id=1, replica_groups=mesh['cam'=8,'tile'=32] {'cam'}, use_global_device_ids=true, to_apply=%region_1.2 | all-reduce | flops 2048 | bytes 16384 | tf_op jit(solution)/shard_map/pmax | solution.py:54
  121.4 14.3 %psum.21 = f32[1,8,256]{2,1,0:T(8,128)S(1)} all-reduce(f32[1,8,256]{2,1,0:T(8,128)S(1)} %bitcast_multiply_fusion), channel_id=1, replica_groups=mesh['cam'=8,'tile'=32] {'cam'}, use_global_device_ids=true, to_apply=%region_3.4 | all-reduce | flops 2048 | bytes 16384 | tf_op jit(solution)/shard_map/psum | solution.py:55
  135.7 9.1 %fusion.1 = f32[8,2048,32]{1,2,0:T(8,128)} fusion(bf16[256,8,32]{0,2,1:T(8,128)(2,1)S(1)} %bitcast.42, f32[8,256,2048]{2,1,0:T(8,128)} %copy-done, f32[8,256]{1,0:T(8,128)S(1)} %add_bitcast_fusion, pred[256,2048]{1,0:T(8,128)(4,1)S(1)} %bitcast.31), kind=kOutput, calls=%fused_computation.6 | convolution fusion | flops 285212672 | bytes 19537920 | tf_op jit(solution)/shard_map/while/body/eval_jaxpr/hqk,qhd->khd/dot_general | solution.py:95
  144.9 28.7 %all-gather.5.cloned.1.call-done = bf16[2048,256]{1,0:T(8,128)(2,1)} async-done(((bf16[64,256]{1,0:T(8,128)(2,1)}), bf16[2048,256]{1,0:T(8,128)(2,1)}) %all-gather.5.cloned.1.call-update) | async-done | bytes 1048592 | tf_op jit(solution)/shard_map/all_gather | solution.py:17
  173.6 1.5 copy.21
  175.1 12.6 %multiply_reduce_fusion = (f32[8,256]{1,0:T(8,128)S(1)}, f32[8,256,2048]{2,1,0:T(8,128)}) fusion(f32[8,256,2048]{2,1,0:T(8,128)} %copy-done, f32[8,256]{1,0:T(8,128)S(1)} %add_bitcast_fusion, pred[256,2048]{1,0:T(8,128)(4,1)S(1)} %bitcast.32, bf16[256,8,32]{0,2,1:T(8,128)(2,1)S(1)} %bitcast.43, bf16[2048,8,32]{0,2,1:T(8,128)(2,1)S(1)} %bitcast.37), kind=kOutput, calls=%fused_computation.1 | convolution fusion | flops 289404928 | bytes 35274752 | tf_op jit(solution)/shard_map/while/body/eval_jaxpr/qhd,khd->hqk/dot_general | solution.py:62
  187.7 12.1 %psum.22 = f32[8,256]{1,0:T(8,128)S(1)} all-reduce(f32[8,256]{1,0:T(8,128)S(1)} %get-tuple-element.60), channel_id=1, replica_groups=mesh['cam'=8,'tile'=32] {'cam'}, use_global_device_ids=true, to_apply=%region_5.6 | all-reduce | flops 2048 | bytes 16384 | tf_op jit(solution)/shard_map/psum | solution.py:71
  199.8 12.2 %multiply_convert_fusion = bf16[8,256,2048]{2,1,0:T(8,128)(2,1)S(1)} fusion(f32[8,256,2048]{2,1,0:T(8,128)} %get-tuple-element.61, f32[8,256,2048]{2,1,0:T(8,128)} %copy-done, f32[8,256]{1,0:T(8,128)S(1)} %psum.22, f32[8,256]{1,0:T(8,128)S(1)} %add_bitcast_fusion, pred[256,2048]{1,0:T(8,128)(4,1)S(1)} %bitcast.33), kind=kLoop, calls=%fused_computation | loop fusion | flops 25165824 | bytes 42483712 | tf_op jit(solution)/shard_map/while/body/eval_jaxpr/convert_element_type | solution.py:76
  212.0 3.2 copy-done.1
  215.2 1.5 convolution_multiply_fusion
  216.7 1.9 copy.23
  218.6 1.9 copy.24
  220.5 4.2 pad_maximum_fusion
  224.8 6.0 %convolution_multiply_fusion.1 = f32[8,256,32]{1,2,0:T(8,128)S(1)} fusion(bf16[8,256,2048]{2,1,0:T(8,128)(2,1)} %copy-done.1, bf16[2048,8,32]{0,2,1:T(8,128)(2,1)S(1)} %bitcast.36), kind=kOutput, calls=%fused_computation.10 | convolution fusion | flops 268500992 | bytes 9699328 | tf_op jit(solution)/shard_map/while/body/eval_jaxpr/hqk,khd->qhd/dot_general | solution.py:80
  230.8 0.1 copy.22
  230.9 33.8 %all-reduce.1 = bf16[256,256]{1,0:T(8,128)(2,1)} all-reduce(f32[256,256]{1,0:T(8,128)S(1)} %copy.22), channel_id=1, replica_groups=mesh['cam'=8,'tile'=32] {'cam'}, use_global_device_ids=true, to_apply=%region_6.7 | all-reduce | flops 65536 | bytes 393216 | tf_op jit(solution)/shard_map/psum | solution.py:106
  264.7 196.6 %reduce-scatter.2.cloned.1.call-done = f32[64,512]{1,0:T(8,128)} async-done(((f32[2048,512]{1,0:T(8,128)}), f32[64,512]{1,0:T(8,128)}) %reduce-scatter.2.cloned.1.call-update) | async-done | bytes 131088 | tf_op jit(solution)/shard_map/reduce_scatter | solution.py:105
  461.3 0.9 convert.4
  462.2 0.6 fusion.10
  (12 shorter events, 0.3 us)
Async XLA Ops:
  7.2 87.1 %all-gather.3.cloned.1.call-start = ((), (), s32[]{:S(2)}) async-start(), calls=%async_computation.1 | async-start | bytes 1081344 | tf_op jit(solution)/shard_map/all_gather | solution.py:16
  7.9 165.7 %all-gather.5.cloned.1.call-start = ((), (), s32[]{:S(2)}) async-start(), calls=%async_computation.2 | async-start | bytes 1081344 | tf_op jit(solution)/shard_map/all_gather | solution.py:17
  8.6 452.6 %reduce-scatter.2.cloned.1.call-start = ((), (), s32[]{:S(2)}) async-start(), calls=%async_computation.3 | async-start | bytes 4325376 | tf_op jit(solution)/shard_map/reduce_scatter | solution.py:105
  99.2 5.7 %copy-start = (f32[8,256,2048]{2,1,0:T(8,128)}, f32[8,256,2048]{2,1,0:T(8,128)S(1)}, u32[]{:S(2)}) copy-start(f32[8,256,2048]{2,1,0:T(8,128)S(1)} %get-tuple-element.59) | copy-start | bytes 50331652
  212.0 3.2 copy-start.1
Sparse Core Ops, SparseCore 0:
  11.4 82.7 all-gather.2
  97.6 75.8 all-gather.4
  224.9 236.3 reduce-scatter.1
where the time goes:
time: 470 us; the launch traced here: 469 us
  waiting for transfers between devices  308 us (66%)
  blocking collectives  72 us (15%)
  matrix products  32.5 us (7%)
  other arithmetic  22.7 us (5%)
  local copies, waits for them, and re-layouts  19.6 us (4%)
  between operations  13.9 us (3%)
    reduce_scatter x1, waiting for transfers between devices, shards(): owned = lax.psum_scatter(joined, 'tile', scatter_dimension=0, tiled=True)  197 us
    all_gather x1, waiting for transfers between devices, shards(): lax.all_gather(keys, 'tile', axis=0, tiled=True)  81.8 us
    psum x1, blocking collectives, shards(): lax.psum(query_parts.reshape(row_count, width), 'cam').astype(jnp.bfloat16)  33.8 us
    all_gather x1, waiting for transfers between devices, shards(): lax.all_gather(values, 'tile', axis=0, tiled=True)  28.7 us
    psum x1, blocking collectives, shards(): lax.psum(local_total * jnp.exp(local_top - global_top), 'cam')  14.3 us
    dot_general x1, matrix products, probs_terms(): jnp.einsum('qhd,khd->hqk', grad_blk, value_mat, preferred_element_type=jn...  12.6 us
    convert_element_type x1, other arithmetic, rounded_terms(): return (probs.astype(jnp.bfloat16), dscores.astype(jnp.bfloat16))  12.2 us
    psum x1, blocking collectives, shards(): delta_all = lax.psum(delta_part, 'cam')  12.1 us
  transfers between devices with their start and end apart: 3, of which 3 were waited for; matrix products, arithmetic and copies ran while one was open for 6% of the time, Pallas kernels for 0%

commit v1 on v0

v1 whole, which is shorter than its diff:
```python
import math

import jax
import jax.numpy as jnp
from jax import lax
from jax.experimental import pallas as pl
from jax.experimental.pallas import tpu as pltpu
from jax.sharding import PartitionSpec as P

NX, NY, NZH, NZL, NC = 4, 4, 2, 4, 2
NZ = NZH * NZL
H = 8
HD = 32
C = H * HD
KB = 32
TQ = 128
NEG = -1e30
BIG = 3e38
SCALE = 1.0 / math.sqrt(HD)
LOG2E = math.log2(math.e)
CH = KB * NX
KEYS = 2 * NY * CH
HALF = KEYS // 2
QB = 2 * TQ
QH = QB // NC
QS = QH // NZL

F32 = jnp.float32
BF16 = jnp.bfloat16


def nt(a, b):
    return lax.dot_general(a, b, (((1,), (1,)), ((), ())), preferred_element_type=F32)


def nn(a, b):
    return jnp.dot(a, b, preferred_element_type=F32)


def remote(src, dst, send, recv, device):
    return pltpu.make_async_remote_copy(
        src_ref=src,
        dst_ref=dst,
        send_sem=send,
        recv_sem=recv,
        device_id=device,
        device_id_type=pl.DeviceIdType.MESH,
    )


def kernel(
    q_in, g_in, k_in, v_in, vis_in, cnt_in,
    gq_out, gk_out, gv_out,
    kv, qd, vis, qs, gs, pbuf, dbuf, cap, kt,
    stat, stat_in, core_out, core_in, alpha, delta,
    dk, dv, rs1_out, rs1_in, rs2_own, rs2_out, rs2_in,
    dqt, dq, dq_sib, dqz_own, dqz_out, dqz_in, dqf_out, dqf_in,
    ga1_s, ga1_r, gb1_s, gb1_r, ga2_s, ga2_r, gb2_s, gb2_r,
    qx_s, qx_r, qc_s, qc_r, vx_s, vx_r,
    st_s, st_r, sc_s, sc_r,
    ra1_s, ra1_r, rb1_s, rb1_r, ra2_s, ra2_r, rb2_s, rb2_r,
    dc_s, dc_r, dz_s, dz_r, df_s, df_r,
):
    cam = lax.axis_index("cam")
    tile = lax.axis_index("tile")
    core = lax.rem(cam, NC)
    zl = lax.div(cam, NC)
    y = lax.rem(tile, NY)
    zh = lax.rem(lax.div(tile, NY), NZH)
    x = lax.div(tile, NY * NZH)
    z = zh * NZL + zl

    def at(x_, y_, z_, core_):
        zh_ = lax.div(z_, NZL)
        zl_ = lax.rem(z_, NZL)
        return {"cam": zl_ * NC + core_, "tile": (x_ * NZH + zh_) * NY + y_}

    def xp(j):
        return at(lax.rem(x + j, NX), y, z, core)

    def yp(j):
        return at(x, lax.rem(y + j, NY), z, core)

    def zp(j):
        return at(x, y, lax.rem(z + j, NZ), core)

    def fp(jz, jc):
        return at(x, y, zh * NZL + lax.rem(zl + jz, NZL), lax.rem(core + jc, NC))

    sibling = fp(0, 1)
    mirror = at(x, y, NZ - 1 - z, core)

    barrier = pltpu.get_barrier_semaphore()
    peers = [xp(j) for j in range(1, NX)] + [yp(j) for j in range(1, NY)] + [zp(j) for j in range(1, NZ)]
    peers += [fp(jz, 1) for jz in range(NZL)]
    for peer in peers:
        pl.semaphore_signal(barrier, inc=1, device_id=peer, device_id_type=pl.DeviceIdType.MESH)

    own_a = pl.multiple_of(y * CH + x * KB, KB)
    own_b = pl.multiple_of(HALF + x * CH + y * KB, KB)
    kv[pl.ds(own_a, KB), :C] = k_in[:KB, :]
    kv[pl.ds(own_a, KB), C:] = v_in[:KB, :]
    kv[pl.ds(own_b, KB), :C] = k_in[KB:, :]
    kv[pl.ds(own_b, KB), C:] = v_in[KB:, :]
    qd[zh, 0] = q_in[...]
    qd[zh, 1] = g_in[...]
    vis[zh, :2, : NX * NZH * NY * 2] = vis_in[...].astype(F32)

    pl.semaphore_wait(barrier, len(peers))

    ga1 = [remote(kv.at[pl.ds(own_a, KB)], kv.at[pl.ds(own_a, KB)], ga1_s.at[j - 1], ga1_r.at[j - 1], xp(j)) for j in range(1, NX)]
    gb1 = [remote(kv.at[pl.ds(own_b, KB)], kv.at[pl.ds(own_b, KB)], gb1_s.at[j - 1], gb1_r.at[j - 1], yp(j)) for j in range(1, NY)]
    for copy in ga1 + gb1:
        copy.start()
    qx = remote(qd.at[zh, core], qd.at[zh, core], qx_s.at[0], qx_r.at[0], mirror)
    qx.start()
    vx = remote(vis.at[zh], vis.at[zh], vx_s.at[0], vx_r.at[0], zp(NZL))
    vx.start()

    head_of = lax.broadcasted_iota(jnp.int32, (QB, C), 1) // HD

    def stack(b):
        qb = qd[b, 0]
        gb = qd[b, 1]

        def one(h, _):
            row = pl.multiple_of((b * H + h) * QB, QB)
            keep = head_of == h
            qs[pl.ds(row, QB), :] = jnp.where(keep, qb, jnp.zeros_like(qb))
            gs[pl.ds(row, QB), :] = jnp.where(keep, gb, jnp.zeros_like(gb))
            return 0

        lax.fori_loop(0, H, one, 0)

    stack(zh)

    chunk_a = pl.multiple_of(y * CH, CH)
    chunk_b = pl.multiple_of(HALF + x * CH, CH)
    for copy in ga1 + gb1:
        copy.wait_recv()
    ga2 = [remote(kv.at[pl.ds(chunk_a, CH)], kv.at[pl.ds(chunk_a, CH)], ga2_s.at[j - 1], ga2_r.at[j - 1], yp(j)) for j in range(1, NY)]
    gb2 = [remote(kv.at[pl.ds(chunk_b, CH)], kv.at[pl.ds(chunk_b, CH)], gb2_s.at[j - 1], gb2_r.at[j - 1], xp(j)) for j in range(1, NX)]
    for copy in ga2 + gb2:
        copy.start()

    blocks = NX * NZH * NY * 2
    row = lax.broadcasted_iota(jnp.int32, (KEYS, blocks), 0)
    col = lax.broadcasted_iota(jnp.int32, (KEYS, blocks), 1)
    half = row // HALF
    outer = (row % HALF) // CH
    inner = (row % CH) // KB
    bx = jnp.where(half == 0, inner, outer)
    by = jnp.where(half == 0, outer, inner)
    block = 2 * ((bx * NZH + zh) * NY + by) + half
    pick = ((block == col) & (row % KB < cnt_in[...])).astype(F32).astype(BF16)
    vx.wait_recv()
    for b in range(NZH):
        seen = jnp.concatenate(
            [jnp.broadcast_to(vis[b, t : t + 1, :blocks], (TQ, blocks)) for t in range(2)], axis=0
        ).astype(BF16)
        cap[b] = jnp.where(nt(pick, seen) > 0.5, BIG, NEG)

    qx.wait_recv()
    qc = remote(qd.at[1 - zh, core], qd.at[1 - zh, core], qc_s.at[0], qc_r.at[0], sibling)
    qc.start()
    for copy in ga2 + gb2:
        copy.wait_recv()
    kt[...] = kv[:, :C].astype(F32).T.astype(BF16)
    qc.wait_recv()
    stack(1 - zh)

    def first(b, lo, hi):
        def one(h, _):
            i = b * H + h
            rows = pl.ds(pl.multiple_of(i * QB, QB), QB)
            s = nt(kv[:, :C], qs[rows, :]) * (SCALE * LOG2E)
            s = jnp.minimum(s, cap[b])
            m = jnp.maximum(jnp.max(s, axis=0, keepdims=True), 0.1 * NEG)
            p = jnp.exp2(s - m)
            pbuf[i] = p
            d = nt(kv[:, C:], gs[rows, :])
            dbuf[i] = d
            stat[b, 0, pl.ds(h, 1), :] = m
            stat[b, 1, pl.ds(h, 1), :] = jnp.sum(p, axis=0, keepdims=True)
            stat[b, 2, pl.ds(h, 1), :] = jnp.sum(p * d, axis=0, keepdims=True)
            return 0

        lax.fori_loop(lo, hi, one, 0)

    def stat_copies(b):
        return [remote(stat.at[b], stat_in.at[b, j - 1], st_s.at[b, j - 1], st_r.at[b, j - 1], zp(j)) for j in range(1, NZ)]

    def core_copy(b):
        return remote(core_out.at[b], core_in.at[b], sc_s.at[b], sc_r.at[b], sibling)

    def merge(parts):
        top = parts[0][0]
        for part in parts[1:]:
            top = jnp.maximum(top, part[0])
        total = jnp.zeros_like(top)
        dot = jnp.zeros_like(top)
        for m, l, d in parts:
            w = jnp.exp2(m - top)
            total = total + l * w
            dot = dot + d * w
        return top, total, dot

    def stat_ring(b):
        for copy in stat_copies(b):
            copy.wait_recv()
        parts = [tuple(stat[b, k] for k in range(3))]
        parts += [tuple(stat_in[b, j, k] for k in range(3)) for j in range(NZ - 1)]
        for k, value in enumerate(merge(parts)):
            core_out[b, k] = value
        core_copy(b).start()

    def stat_final(b):
        core_copy(b).wait_recv()
        top, total, dot = merge([tuple(core_out[b, k] for k in range(3)), tuple(core_in[b, k] for k in range(3))])
        inv = 1.0 / total
        alpha[b] = jnp.exp2(stat[b, 0] - top) * inv
        delta[b] = dot * inv

    def chunk_copies(i):
        return (
            remote(rs1_out.at[i, 0], rs1_in.at[i, 0], ra1_s.at[i], ra1_r.at[i], yp(i + 1)),
            remote(rs1_out.at[i, 1], rs1_in.at[i, 1], rb1_s.at[i], rb1_r.at[i], xp(i + 1)),
        )

    def second(b, lo, hi):
        stack_rows = pl.ds(b * H * QB, H * QB)

        def one(i, _):
            ra = pl.ds(pl.multiple_of(lax.rem(y + 1 + i, NY) * CH, CH), CH)
            rb = pl.ds(pl.multiple_of(HALF + lax.rem(x + 1 + i, NX) * CH, CH), CH)
            ps = []
            ts = []
            dqs = []
            ktc = jnp.concatenate([kt[:, ra], kt[:, rb]], axis=1)
            for h in range(H):
                n = b * H + h
                a = alpha[b, h : h + 1, :]
                e = delta[b, h : h + 1, :]
                p = jnp.concatenate([pbuf[n, ra, :], pbuf[n, rb, :]], axis=0) * a
                d = jnp.concatenate([dbuf[n, ra, :], dbuf[n, rb, :]], axis=0)
                t = (p * (d - e)).astype(BF16)
                ps.append(p.astype(BF16))
                ts.append(t)
                dqs.append(nn(ktc[h * HD : (h + 1) * HD, :], t))
            dqc = jnp.concatenate(dqs, axis=0)
            dkc = nn(jnp.concatenate(ts, axis=1), qs[stack_rows, :])
            dvc = nn(jnp.concatenate(ps, axis=1), gs[stack_rows, :])
            if b == 0:
                dk[i] = dkc
                dv[i] = dvc
            else:
                dkc = dk[i] + dkc
                dvc = dv[i] + dvc

                @pl.when(i < NX - 1)
                def _():
                    rs1_out[i, 0, :, :C] = dkc[:CH].astype(BF16)
                    rs1_out[i, 1, :, :C] = dkc[CH:].astype(BF16)
                    rs1_out[i, 0, :, C:] = dvc[:CH].astype(BF16)
                    rs1_out[i, 1, :, C:] = dvc[CH:].astype(BF16)
                    for copy in chunk_copies(i):
                        copy.start()

                @pl.when(i == NX - 1)
                def _():
                    dk[i] = dkc
                    dv[i] = dvc

            @pl.when(i == 0)
            def _():
                dqt[b] = dqc

            @pl.when(i > 0)
            def _():
                dqt[b] = dqt[b] + dqc

            return 0

        lax.fori_loop(lo, hi, one, 0)

    other_half = pl.ds(pl.multiple_of((1 - core) * QH, QH), QH)

    def dq_core(b):
        return remote(dq.at[b, other_half], dq_sib.at[b], dc_s.at[b], dc_r.at[b], sibling)

    def dq_start(b):
        dq[b] = dqt[b].T * SCALE
        dq_core(b).start()

    def dq_slot(b, j):
        return remote(
            dqz_out.at[b, pl.ds(j * QS, QS)],
            dqz_in.at[z],
            dz_s.at[b * NZL + j],
            dz_r.at[z],
            at(x, y, b * NZL + j, core),
        )

    def dq_ring(b):
        dq_core(b).wait_recv()
        mine = dq[b, pl.ds(pl.multiple_of(core * QH, QH), QH), :] + dq_sib[b]
        dqz_out[b] = mine.astype(BF16)
        for j in range(NZL):

            @pl.when(z == b * NZL + j)
            def _(j=j):
                dqz_own[...] = mine[j * QS : (j + 1) * QS, :]

            @pl.when(z != b * NZL + j)
            def _(j=j):
                dq_slot(b, j).start()

    first(0, 0, H)
    for copy in stat_copies(0):
        copy.start()
    first(1, 0, H // 2)
    stat_ring(0)
    first(1, H // 2, H)
    for copy in stat_copies(1):
        copy.start()
    stat_final(0)
    second(0, 0, NX // 2)
    stat_ring(1)
    second(0, NX // 2, NX)
    dq_start(0)
    stat_final(1)
    second(1, 0, NX // 2)
    dq_ring(0)
    second(1, NX // 2, NX)
    dq_start(1)

    for i in range(NX - 1):
        for copy in chunk_copies(i):
            copy.wait_recv()
    for half in range(2):
        for part, acc in enumerate((dk, dv)):
            cols = slice(part * C, (part + 1) * C)
            total = acc[NX - 1, half * CH : (half + 1) * CH, :]
            for i in range(NX - 1):
                total = total + rs1_in[i, half, :, cols].astype(F32)
            rs2_own[half, :, cols] = total
            rs2_out[half, :, cols] = total.astype(BF16)

    def rs2_copies(j):
        rows_a = pl.ds(pl.multiple_of(lax.rem(x + j, NX) * KB, KB), KB)
        rows_b = pl.ds(pl.multiple_of(lax.rem(y + j, NY) * KB, KB), KB)
        return (
            remote(rs2_out.at[0, rows_a], rs2_in.at[j - 1, 0], ra2_s.at[j - 1], ra2_r.at[j - 1], xp(j)),
            remote(rs2_out.at[1, rows_b], rs2_in.at[j - 1, 1], rb2_s.at[j - 1], rb2_r.at[j - 1], yp(j)),
        )

    for j in range(1, NX):
        for copy in rs2_copies(j):
            copy.start()

    dq_ring(1)
    total = dqz_own[...]
    for j in range(1, NZ):
        sender = lax.rem(z + j, NZ)
        remote(dqz_out.at[0, pl.ds(0, QS)], dqz_in.at[sender], dz_s.at[0], dz_r.at[sender], sibling).wait_recv()
        total = total + dqz_in[sender].astype(F32)
    dqf_out[...] = total.astype(BF16)

    def dqf_copy(jz, jc):
        k = jz * NC + jc - 1
        return remote(dqf_out, dqf_in.at[k], df_s.at[k], df_r.at[k], fp(jz, jc))

    others = [(jz, jc) for jz in range(NZL) for jc in range(NC) if jz + jc > 0]
    for jz, jc in others:
        dqf_copy(jz, jc).start()
    gq_out[pl.ds(pl.multiple_of(core * QH + zl * QS, QS), QS), :] = dqf_out[...]

    for j in range(1, NX):
        for copy in rs2_copies(j):
            copy.wait_recv()
    for half, pos in ((0, x), (1, y)):
        rows = pl.ds(pl.multiple_of(pos * KB, KB), KB)
        total = rs2_own[half, rows, :]
        for j in range(NX - 1):
            total = total + rs2_in[j, half].astype(F32)
        gk_out[half * KB : (half + 1) * KB, :] = (total[:, :C] * SCALE).astype(BF16)
        gv_out[half * KB : (half + 1) * KB, :] = total[:, C:].astype(BF16)

    for jz, jc in others:
        dqf_copy(jz, jc).wait_recv()
        fz = lax.rem(zl - jz + NZL, NZL)
        fc = lax.rem(core - jc + NC, NC)
        gq_out[pl.ds(pl.multiple_of(fc * QH + fz * QS, QS), QS), :] = dqf_in[jz * NC + jc - 1]

    for copy in ga1 + gb1 + ga2 + gb2 + [qx, vx, qc]:
        copy.wait_send()
    for b in range(NZH):
        for copy in stat_copies(b):
            copy.wait_send()
        core_copy(b).wait_send()
        dq_core(b).wait_send()
        for j in range(NZL):

            @pl.when(z != b * NZL + j)
            def _(b=b, j=j):
                dq_slot(b, j).wait_send()

    for i in range(NX - 1):
        for copy in chunk_copies(i):
            copy.wait_send()
    for j in range(1, NX):
        for copy in rs2_copies(j):
            copy.wait_send()
    for jz, jc in others:
        dqf_copy(jz, jc).wait_send()


def shards(queries, keys, values, grad_out, visible, counts):
    vmem = pl.BlockSpec(memory_space=pltpu.VMEM)
    dma = pltpu.SemaphoreType.DMA
    V = pltpu.VMEM
    scratch = [
        V((KEYS, 2 * C), BF16),
        V((NZH, 2, QB, C), BF16),
        V((NZH, 8, 128), F32),
        V((NZH * H * QB, C), BF16),
        V((NZH * H * QB, C), BF16),
        V((NZH * H, KEYS, QB), F32),
        V((NZH * H, KEYS, QB), F32),
        V((NZH, KEYS, QB), F32),
        V((C, KEYS), BF16),
        V((NZH, 3, H, QB), F32),
        V((NZH, NZ - 1, 3, H, QB), F32),
        V((NZH, 3, H, QB), F32),
        V((NZH, 3, H, QB), F32),
        V((NZH, H, QB), F32),
        V((NZH, H, QB), F32),
        V((NX, 2 * CH, C), F32),
        V((NX, 2 * CH, C), F32),
        V((NX - 1, 2, CH, 2 * C), BF16),
        V((NX - 1, 2, CH, 2 * C), BF16),
        V((2, CH, 2 * C), F32),
        V((2, CH, 2 * C), BF16),
        V((NX - 1, 2, KB, 2 * C), BF16),
        V((NZH, C, QB), F32),
        V((NZH, QB, C), F32),
        V((NZH, QH, C), F32),
        V((QS, C), F32),
        V((NZH, QH, C), BF16),
        V((NZ, QS, C), BF16),
        V((QS, C), BF16),
        V((NZL * NC - 1, QS, C), BF16),
    ]
    sems = [(NX - 1,)] * 8 + [(1,)] * 6 + [(NZH, NZ - 1)] * 2 + [(NZH,)] * 2 + [(NX - 1,)] * 8
    sems += [(NZH,)] * 2 + [(NZ,)] * 2 + [(NZL * NC - 1,)] * 2
    scratch += [dma(s) for s in sems]
    return pl.pallas_call(
        kernel,
        out_shape=(
            jax.ShapeDtypeStruct((QB, C), BF16),
            jax.ShapeDtypeStruct((2 * KB, C), BF16),
            jax.ShapeDtypeStruct((2 * KB, C), BF16),
        ),
        in_specs=[vmem] * 6,
        out_specs=(vmem,) * 3,
        scratch_shapes=scratch,
        compiler_params=pltpu.CompilerParams(
            collective_id=0, has_side_effects=True, vmem_limit_bytes=60 * 1024 * 1024
        ),
    )(queries, grad_out, keys, values, visible, counts.reshape(1, -1))


def solution(mesh):
    in_specs = (
        P("tile", None),
        P(("cam", "tile"), None),
        P(("cam", "tile"), None),
        P("tile", None),
        P("tile", "cam"),
        P("cam"),
    )
    out_specs = (P("tile", None), P(("cam", "tile"), None), P(("cam", "tile"), None))
    return jax.shard_map(shards, mesh=mesh, in_specs=in_specs, out_specs=out_specs, check_vma=False)
```

time: 470 us -> 67.2 us (0.14)
  the two profiles are of different devices: /device:TPU:32 before, /device:TPU:1 now
where the time goes in v1:
time: 67.2 us; the launch traced here: 66.1 us
  Pallas kernels  62.5 us (93%)
  local copies, waits for them, and re-layouts  2.96 us (4%)
    pallas_call x1, Pallas kernels, shards(): pl.pallas_call(kernel, out_shape=(jax.ShapeDtypeStruct((QB, C), BF16), ja...  62.5 us
    unnamed x7, local copies, waits for them, and re-layouts  2.96 us

profile of v1, /device:TPU:1, one launch (start us, length us, event | category | flops | bytes accessed | tf_op | source)
XLA Modules:
  0.0 66.1 jit_solution(4228506532913207405)
XLA Ops:
  0.6 62.5 %shard_map.85 = (bf16[256,256]{1,0:T(8,128)(2,1)}, bf16[64,256]{1,0:T(8,128)(2,1)}, bf16[64,256]{1,0:T(8,128)(2,1)}) custom-call(bf16[256,256]{1,0:T(8,128)(2,1)} %q_in.1, bf16[256,256]{1,0:T(8,128)(2,1)} %g_in.1, bf16[64,256]{1,0:T(8,128)(2,1)} %k_in.1, bf16[64,256]{1,0:T(8,128)(2,1)} %v_in.1, s32[2,64]{1,0:T(2,128)} %vis_in.1, s32[1,64]{1,0:T(1,128)} %bitcast.1), custom_call_target="tpu_custom_call" | custom-call | tf_op jit(solution)/shard_map/pallas_call | solution.py:457
  63.1 0.0 copy-start.1
  63.1 1.6 %copy.12 = bf16[256,256]{1,0:T(8,128)(2,1)} copy(bf16[256,256]{1,0:T(8,128)(2,1)} %get-tuple-element.6) | data formatting | bytes 262144
  64.7 0.0 copy-done.1
  64.7 0.0 copy-start
  64.7 0.6 copy.13
  65.3 0.2 copy-done
  65.5 0.6 copy.14
Async XLA Ops:
  63.1 1.6 %copy-start.1 = (bf16[64,256]{1,0:T(8,128)(2,1)S(1)}, bf16[64,256]{1,0:T(8,128)(2,1)}, u32[]{:S(2)}) copy-start(bf16[64,256]{1,0:T(8,128)(2,1)} %get-tuple-element.7) | copy-start | bytes 98308
  64.7 0.8 %copy-start = (bf16[64,256]{1,0:T(8,128)(2,1)S(1)}, bf16[64,256]{1,0:T(8,128)(2,1)}, u32[]{:S(2)}) copy-start(bf16[64,256]{1,0:T(8,128)(2,1)} %get-tuple-element.8) | copy-start | bytes 98308

commit v2 on v1

--- a/solution.py
+++ b/solution.py
@@ -52,7 +52,7 @@
     q_in, g_in, k_in, v_in, vis_in, cnt_in,
     gq_out, gk_out, gv_out,
     kv, qd, vis, qs, gs, pbuf, dbuf, cap, kt,
-    stat, stat_in, core_out, core_in, alpha, delta,
+    cstat, stat, stat_in, core_out, core_in, alpha, delta,
     dk, dv, rs1_out, rs1_in, rs2_own, rs2_out, rs2_in,
     dqt, dq, dq_sib, dqz_own, dqz_out, dqz_in, dqf_out, dqf_in,
     ga1_s, ga1_r, gb1_s, gb1_r, ga2_s, ga2_r, gb2_s, gb2_r,
@@ -134,15 +134,6 @@
 
     stack(zh)
 
-    chunk_a = pl.multiple_of(y * CH, CH)
-    chunk_b = pl.multiple_of(HALF + x * CH, CH)
-    for copy in ga1 + gb1:
-        copy.wait_recv()
-    ga2 = [remote(kv.at[pl.ds(chunk_a, CH)], kv.at[pl.ds(chunk_a, CH)], ga2_s.at[j - 1], ga2_r.at[j - 1], yp(j)) for j in range(1, NY)]
-    gb2 = [remote(kv.at[pl.ds(chunk_b, CH)], kv.at[pl.ds(chunk_b, CH)], gb2_s.at[j - 1], gb2_r.at[j - 1], xp(j)) for j in range(1, NX)]
-    for copy in ga2 + gb2:
-        copy.start()
-
     blocks = NX * NZH * NY * 2
     row = lax.broadcasted_iota(jnp.int32, (KEYS, blocks), 0)
     col = lax.broadcasted_iota(jnp.int32, (KEYS, blocks), 1)
@@ -153,47 +144,53 @@
     by = jnp.where(half == 0, outer, inner)
     block = 2 * ((bx * NZH + zh) * NY + by) + half
     pick = ((block == col) & (row % KB < cnt_in[...])).astype(F32).astype(BF16)
-    vx.wait_recv()
-    for b in range(NZH):
+
+    def cap_of(b):
         seen = jnp.concatenate(
             [jnp.broadcast_to(vis[b, t : t + 1, :blocks], (TQ, blocks)) for t in range(2)], axis=0
         ).astype(BF16)
         cap[b] = jnp.where(nt(pick, seen) > 0.5, BIG, NEG)
 
-    qx.wait_recv()
-    qc = remote(qd.at[1 - zh, core], qd.at[1 - zh, core], qc_s.at[0], qc_r.at[0], sibling)
-    qc.start()
-    for copy in ga2 + gb2:
+    cap_of(zh)
+
+    chunk_a = pl.multiple_of(y * CH, CH)
+    chunk_b = pl.multiple_of(HALF + x * CH, CH)
+    for copy in ga1 + gb1:
         copy.wait_recv()
-    kt[...] = kv[:, :C].astype(F32).T.astype(BF16)
-    qc.wait_recv()
-    stack(1 - zh)
-
-    def first(b, lo, hi):
-        def one(h, _):
-            i = b * H + h
-            rows = pl.ds(pl.multiple_of(i * QB, QB), QB)
-            s = nt(kv[:, :C], qs[rows, :]) * (SCALE * LOG2E)
-            s = jnp.minimum(s, cap[b])
+    ga2 = [remote(kv.at[pl.ds(chunk_a, CH)], kv.at[pl.ds(chunk_a, CH)], ga2_s.at[j - 1], ga2_r.at[j - 1], yp(j)) for j in range(1, NY)]
+    gb2 = [remote(kv.at[pl.ds(chunk_b, CH)], kv.at[pl.ds(chunk_b, CH)], gb2_s.at[j - 1], gb2_r.at[j - 1], xp(j)) for j in range(1, NX)]
+    for j in (0, 2, 1):
+        ga2[j].start()
+        gb2[j].start()
+
+    def chunk_rows(i):
+        ra = pl.ds(pl.multiple_of(lax.rem(y + 1 + i, NY) * CH, CH), CH)
+        rb = pl.ds(pl.multiple_of(HALF + lax.rem(x + 1 + i, NX) * CH, CH), CH)
+        return ra, rb
+
+    def first(b, i):
+        ra, rb = chunk_rows(i)
+        kc = jnp.concatenate([kv[ra, :C], kv[rb, :C]], axis=0)
+        vc = jnp.concatenate([kv[ra, C:], kv[rb, C:]], axis=0)
+        n = b * NX + i
+        for h in range(H):
+            rows = pl.ds(pl.multiple_of((b * H + h) * QB, QB), QB)
+            s = nt(kc, qs[rows, :]) * (SCALE * LOG2E)
+            s = jnp.minimum(s, jnp.concatenate([cap[b, ra, :], cap[b, rb, :]], axis=0))
             m = jnp.maximum(jnp.max(s, axis=0, keepdims=True), 0.1 * NEG)
             p = jnp.exp2(s - m)
-            pbuf[i] = p
-            d = nt(kv[:, C:], gs[rows, :])
-            dbuf[i] = d
-            stat[b, 0, pl.ds(h, 1), :] = m
-            stat[b, 1, pl.ds(h, 1), :] = jnp.sum(p, axis=0, keepdims=True)
-            stat[b, 2, pl.ds(h, 1), :] = jnp.sum(p * d, axis=0, keepdims=True)
-            return 0
-
-        lax.fori_loop(lo, hi, one, 0)
+            pbuf[n, h] = p
+            d = nt(vc, gs[rows, :])
+            dbuf[n, h] = d
+            cstat[n, 0, h : h + 1, :] = m
+            cstat[n, 1, h : h + 1, :] = jnp.sum(p, axis=0, keepdims=True)
+            cstat[n, 2, h : h + 1, :] = jnp.sum(p * d, axis=0, keepdims=True)
 
     def stat_copies(b):
         return [remote(stat.at[b], stat_in.at[b, j - 1], st_s.at[b, j - 1], st_r.at[b, j - 1], zp(j)) for j in range(1, NZ)]
 
-    def core_copy(b):
-        return remote(core_out.at[b], core_in.at[b], sc_s.at[b], sc_r.at[b], sibling)
-
-    def merge(parts):
+    def stat_send(b):
+        parts = [tuple(cstat[b * NX + i, k] for k in range(3)) for i in range(NX)]
         top = parts[0][0]
         for part in parts[1:]:
             top = jnp.maximum(top, part[0])
@@ -203,23 +200,42 @@
             w = jnp.exp2(m - top)
             total = total + l * w
             dot = dot + d * w
-        return top, total, dot
+        total = jnp.maximum(total, 1e-30)
+        stat[b, 0] = top + jnp.log2(total)
+        stat[b, 1] = dot / total
+        for copy in stat_copies(b):
+            copy.start()
+
+    def core_copy(b):
+        return remote(core_out.at[b], core_in.at[b], sc_s.at[b], sc_r.at[b], sibling)
+
+    def merge(parts):
+        top = parts[0][0]
+        for part in parts[1:]:
+            top = jnp.maximum(top, part[0])
+        total = jnp.zeros_like(top)
+        dot = jnp.zeros_like(top)
+        for lse, mean in parts:
+            w = jnp.exp2(lse - top)
+            total = total + w
+            dot = dot + mean * w
+        return top + jnp.log2(total), dot / total
 
     def stat_ring(b):
         for copy in stat_copies(b):
             copy.wait_recv()
-        parts = [tuple(stat[b, k] for k in range(3))]
-        parts += [tuple(stat_in[b, j, k] for k in range(3)) for j in range(NZ - 1)]
+        parts = [(stat[b, 0], stat[b, 1])]
+        parts += [(stat_in[b, j, 0], stat_in[b, j, 1]) for j in range(NZ - 1)]
         for k, value in enumerate(merge(parts)):
             core_out[b, k] = value
         core_copy(b).start()
 
     def stat_final(b):
         core_copy(b).wait_recv()
-        top, total, dot = merge([tuple(core_out[b, k] for k in range(3)), tuple(core_in[b, k] for k in range(3))])
-        inv = 1.0 / total
-        alpha[b] = jnp.exp2(stat[b, 0] - top) * inv
-        delta[b] = dot * inv
+        lse, mean = merge([(core_out[b, 0], core_out[b, 1]), (core_in[b, 0], core_in[b, 1])])
+        for i in range(NX):
+            alpha[b * NX + i] = jnp.exp2(cstat[b * NX + i, 0] - lse)
+        delta[b] = mean
 
     def chunk_copies(i):
         return (
@@ -231,22 +247,19 @@
         stack_rows = pl.ds(b * H * QB, H * QB)
 
         def one(i, _):
-            ra = pl.ds(pl.multiple_of(lax.rem(y + 1 + i, NY) * CH, CH), CH)
-            rb = pl.ds(pl.multiple_of(HALF + lax.rem(x + 1 + i, NX) * CH, CH), CH)
+            n = b * NX + i
             ps = []
             ts = []
             dqs = []
-            ktc = jnp.concatenate([kt[:, ra], kt[:, rb]], axis=1)
             for h in range(H):
-                n = b * H + h
-                a = alpha[b, h : h + 1, :]
+                a = alpha[n, h : h + 1, :]
                 e = delta[b, h : h + 1, :]
-                p = jnp.concatenate([pbuf[n, ra, :], pbuf[n, rb, :]], axis=0) * a
-                d = jnp.concatenate([dbuf[n, ra, :], dbuf[n, rb, :]], axis=0)
+                p = pbuf[n, h] * a
+                d = dbuf[n, h]
                 t = (p * (d - e)).astype(BF16)
                 ps.append(p.astype(BF16))
                 ts.append(t)
-                dqs.append(nn(ktc[h * HD : (h + 1) * HD, :], t))
+                dqs.append(nn(kt[i, h * HD : (h + 1) * HD, :], t))
             dqc = jnp.concatenate(dqs, axis=0)
             dkc = nn(jnp.concatenate(ts, axis=1), qs[stack_rows, :])
             dvc = nn(jnp.concatenate(ps, axis=1), gs[stack_rows, :])
@@ -315,14 +328,41 @@
             def _(j=j):
                 dq_slot(b, j).start()
 
-    first(0, 0, H)
-    for copy in stat_copies(0):
-        copy.start()
-    first(1, 0, H // 2)
+    first(zh, NX - 1)
+    vx.wait_recv()
+    cap_of(1 - zh)
+    qx.wait_recv()
+    qc = remote(qd.at[1 - zh, core], qd.at[1 - zh, core], qc_s.at[0], qc_r.at[0], sibling)
+    qc.start()
+    qc.wait_recv()
+    stack(1 - zh)
+
+    def unit(n, _):
+        for step, j in enumerate((2, 0, 1)):
+
+            @pl.when(n == step)
+            def _(j=j):
+                ga2[j].wait_recv()
+                gb2[j].wait_recv()
+
+        in_0 = NX - 1 + zh
+        b = (n >= in_0).astype(jnp.int32)
+        place = jnp.where(b == 0, n + 1 - zh, n - in_0 + zh)
+        i = jnp.where(place == 0, NX - 1, jnp.where(place == 1, 0, jnp.where(place == 2, 2, 1)))
+        first(b, i)
+
+        @pl.when(n == in_0 - 1)
+        def _():
+            stat_send(0)
+
+        return 0
+
+    lax.fori_loop(0, NZH * NX - 1, unit, 0)
+    stat_send(1)
+    for i in range(NX):
+        ra, rb = chunk_rows(i)
+        kt[i] = jnp.concatenate([kv[ra, :C], kv[rb, :C]], axis=0).astype(F32).T.astype(BF16)
     stat_ring(0)
-    first(1, H // 2, H)
-    for copy in stat_copies(1):
-        copy.start()
     stat_final(0)
     second(0, 0, NX // 2)
     stat_ring(1)
@@ -425,15 +465,16 @@
         V((NZH, 8, 128), F32),
         V((NZH * H * QB, C), BF16),
         V((NZH * H * QB, C), BF16),
-        V((NZH * H, KEYS, QB), F32),
-        V((NZH * H, KEYS, QB), F32),
+        V((NZH * NX, H, 2 * CH, QB), F32),
+        V((NZH * NX, H, 2 * CH, QB), F32),
         V((NZH, KEYS, QB), F32),
-        V((C, KEYS), BF16),
-        V((NZH, 3, H, QB), F32),
-        V((NZH, NZ - 1, 3, H, QB), F32),
-        V((NZH, 3, H, QB), F32),
-        V((NZH, 3, H, QB), F32),
-        V((NZH, H, QB), F32),
+        V((NX, C, 2 * CH), BF16),
+        V((NZH * NX, 3, H, QB), F32),
+        V((NZH, 2, H, QB), F32),
+        V((NZH, NZ - 1, 2, H, QB), F32),
+        V((NZH, 2, H, QB), F32),
+        V((NZH, 2, H, QB), F32),
+        V((NZH * NX, H, QB), F32),
         V((NZH, H, QB), F32),
         V((NX, 2 * CH, C), F32),
         V((NX, 2 * CH, C), F32),

time: 67.2 us -> 58.6 us (0.87)
  Pallas kernels: 62.5 us -> 54.4 us
    pallas_call x1, Pallas kernels: 62.5 us -> 54.4 us  [shards(): pl.pallas_call(kernel, out_shape=(jax.ShapeDtypeStruct((QB, C), BF16), ja...]
where the time goes in v2:
time: 58.6 us; the launch traced here: 58 us
  Pallas kernels  54.4 us (93%)
  local copies, waits for them, and re-layouts  2.96 us (5%)
  between operations  0.65 us (1%)
    pallas_call x1, Pallas kernels, shards(): pl.pallas_call(kernel, out_shape=(jax.ShapeDtypeStruct((QB, C), BF16), ja...  54.4 us
    unnamed x7, local copies, waits for them, and re-layouts  2.96 us

profile of v2, /device:TPU:1, one launch (start us, length us, event | category | flops | bytes accessed | tf_op | source)
XLA Modules:
  0.0 58.0 jit_solution(5448672325628978413)
XLA Ops:
  0.6 54.4 %shard_map.85 = (bf16[256,256]{1,0:T(8,128)(2,1)}, bf16[64,256]{1,0:T(8,128)(2,1)}, bf16[64,256]{1,0:T(8,128)(2,1)}) custom-call(bf16[256,256]{1,0:T(8,128)(2,1)} %q_in.1, bf16[256,256]{1,0:T(8,128)(2,1)} %g_in.1, bf16[64,256]{1,0:T(8,128)(2,1)} %k_in.1, bf16[64,256]{1,0:T(8,128)(2,1)} %v_in.1, s32[2,64]{1,0:T(2,128)} %vis_in.1, s32[1,64]{1,0:T(1,128)} %bitcast.1), custom_call_target="tpu_custom_call" | custom-call | tf_op jit(solution)/shard_map/pallas_call | solution.py:498
  55.1 0.0 copy-start.1
  55.1 1.6 %copy.12 = bf16[256,256]{1,0:T(8,128)(2,1)} copy(bf16[256,256]{1,0:T(8,128)(2,1)} %get-tuple-element.6) | data formatting | bytes 262144
  56.6 0.0 copy-done.1
  56.6 0.0 copy-start
  56.6 0.6 %copy.13 = bf16[64,256]{1,0:T(8,128)(2,1)} copy(bf16[64,256]{1,0:T(8,128)(2,1)S(1)} %copy-done.1) | data formatting | bytes 65536
  57.3 0.2 copy-done
  57.4 0.6 %copy.14 = bf16[64,256]{1,0:T(8,128)(2,1)} copy(bf16[64,256]{1,0:T(8,128)(2,1)S(1)} %copy-done) | data formatting | bytes 65536
Async XLA Ops:
  55.1 1.6 %copy-start.1 = (bf16[64,256]{1,0:T(8,128)(2,1)S(1)}, bf16[64,256]{1,0:T(8,128)(2,1)}, u32[]{:S(2)}) copy-start(bf16[64,256]{1,0:T(8,128)(2,1)} %get-tuple-element.7) | copy-start | bytes 98308
  56.6 0.8 %copy-start = (bf16[64,256]{1,0:T(8,128)(2,1)S(1)}, bf16[64,256]{1,0:T(8,128)(2,1)}, u32[]{:S(2)}) copy-start(bf16[64,256]{1,0:T(8,128)(2,1)} %get-tuple-element.8) | copy-start | bytes 98308

commit v3 on v2

--- a/solution.py
+++ b/solution.py
@@ -51,7 +51,7 @@
 def kernel(
     q_in, g_in, k_in, v_in, vis_in, cnt_in,
     gq_out, gk_out, gv_out,
-    kv, qd, vis, qs, gs, pbuf, dbuf, cap, kt,
+    vis_i, cnt, pb, tb, in_s, kv, qd, vis, qs, gs, pbuf, dbuf, cap, kt,
     cstat, stat, stat_in, core_out, core_in, alpha, delta,
     dk, dv, rs1_out, rs1_in, rs2_own, rs2_out, rs2_in,
     dqt, dq, dq_sib, dqz_own, dqz_out, dqz_in, dqf_out, dqf_in,
@@ -98,13 +98,22 @@
 
     own_a = pl.multiple_of(y * CH + x * KB, KB)
     own_b = pl.multiple_of(HALF + x * CH + y * KB, KB)
-    kv[pl.ds(own_a, KB), :C] = k_in[:KB, :]
-    kv[pl.ds(own_a, KB), C:] = v_in[:KB, :]
-    kv[pl.ds(own_b, KB), :C] = k_in[KB:, :]
-    kv[pl.ds(own_b, KB), C:] = v_in[KB:, :]
-    qd[zh, 0] = q_in[...]
-    qd[zh, 1] = g_in[...]
-    vis[zh, :2, : NX * NZH * NY * 2] = vis_in[...].astype(F32)
+    loads = [
+        (k_in.at[pl.ds(0, KB)], kv.at[pl.ds(own_a, KB), pl.ds(0, C)]),
+        (v_in.at[pl.ds(0, KB)], kv.at[pl.ds(own_a, KB), pl.ds(C, C)]),
+        (k_in.at[pl.ds(KB, KB)], kv.at[pl.ds(own_b, KB), pl.ds(0, C)]),
+        (v_in.at[pl.ds(KB, KB)], kv.at[pl.ds(own_b, KB), pl.ds(C, C)]),
+        (q_in, qd.at[zh, 0]),
+        (g_in, qd.at[zh, 1]),
+        (vis_in, vis_i),
+        (cnt_in, cnt),
+    ]
+    loads = [pltpu.make_async_copy(src, dst, in_s.at[n]) for n, (src, dst) in enumerate(loads)]
+    for copy in loads:
+        copy.start()
+    for copy in loads:
+        copy.wait()
+    vis[zh, :2, : NX * NZH * NY * 2] = vis_i[...].astype(F32)
 
     pl.semaphore_wait(barrier, len(peers))
 
@@ -143,7 +152,7 @@
     bx = jnp.where(half == 0, inner, outer)
     by = jnp.where(half == 0, outer, inner)
     block = 2 * ((bx * NZH + zh) * NY + by) + half
-    pick = ((block == col) & (row % KB < cnt_in[...])).astype(F32).astype(BF16)
+    pick = ((block == col) & (row % KB < cnt[...])).astype(F32).astype(BF16)
 
     def cap_of(b):
         seen = jnp.concatenate(
@@ -243,54 +252,63 @@
             remote(rs1_out.at[i, 1], rs1_in.at[i, 1], rb1_s.at[i], rb1_r.at[i], xp(i + 1)),
         )
 
-    def second(b, lo, hi):
-        stack_rows = pl.ds(b * H * QB, H * QB)
-
+    def prepare(b, i, first_chunk):
+        n = b * NX + i
+        rows = pl.ds(pl.multiple_of(i * 2 * CH, 2 * CH), 2 * CH)
+        dqs = []
+        for h in range(H):
+            a = alpha[n, h : h + 1, :]
+            e = delta[b, h : h + 1, :]
+            p = pbuf[n, h] * a
+            t = (p * (dbuf[n, h] - e)).astype(BF16)
+            pb[rows, h * QB : (h + 1) * QB] = p.astype(BF16)
+            tb[rows, h * QB : (h + 1) * QB] = t
+            dqs.append(nn(kt[i, h * HD : (h + 1) * HD, :], t))
+        dqc = jnp.concatenate(dqs, axis=0)
+
+        @pl.when(first_chunk)
+        def _():
+            dqt[b] = dqc
+
+        @pl.when(jnp.logical_not(first_chunk))
+        def _():
+            dqt[b] = dqt[b] + dqc
+
+    def prepare_0():
         def one(i, _):
-            n = b * NX + i
-            ps = []
-            ts = []
-            dqs = []
-            for h in range(H):
-                a = alpha[n, h : h + 1, :]
-                e = delta[b, h : h + 1, :]
-                p = pbuf[n, h] * a
-                d = dbuf[n, h]
-                t = (p * (d - e)).astype(BF16)
-                ps.append(p.astype(BF16))
-                ts.append(t)
-                dqs.append(nn(kt[i, h * HD : (h + 1) * HD, :], t))
-            dqc = jnp.concatenate(dqs, axis=0)
-            dkc = nn(jnp.concatenate(ts, axis=1), qs[stack_rows, :])
-            dvc = nn(jnp.concatenate(ps, axis=1), gs[stack_rows, :])
-            if b == 0:
-                dk[i] = dkc
-                dv[i] = dvc
-            else:
-                dkc = dk[i] + dkc
-                dvc = dv[i] + dvc
-
-                @pl.when(i < NX - 1)
-                def _():
-                    rs1_out[i, 0, :, :C] = dkc[:CH].astype(BF16)
-                    rs1_out[i, 1, :, :C] = dkc[CH:].astype(BF16)
-                    rs1_out[i, 0, :, C:] = dvc[:CH].astype(BF16)
-                    rs1_out[i, 1, :, C:] = dvc[CH:].astype(BF16)
-                    for copy in chunk_copies(i):
-                        copy.start()
-
-                @pl.when(i == NX - 1)
-                def _():
-                    dk[i] = dkc
-                    dv[i] = dvc
-
-            @pl.when(i == 0)
+            prepare(0, i, i == 0)
+            return 0
+
+        lax.fori_loop(0, NX, one, 0)
+
+    def grads_0(pair):
+        rows = slice(pair * 4 * CH, (pair + 1) * 4 * CH)
+        dkc = nn(tb[rows, :], qs[: H * QB, :])
+        dvc = nn(pb[rows, :], gs[: H * QB, :])
+        for u in range(2):
+            dk[2 * pair + u] = dkc[u * 2 * CH : (u + 1) * 2 * CH]
+            dv[2 * pair + u] = dvc[u * 2 * CH : (u + 1) * 2 * CH]
+
+    def second_1(lo, hi):
+        def one(n, _):
+            i = jnp.where(n < 2, 1 - n, n)
+            rows = pl.ds(pl.multiple_of(i * 2 * CH, 2 * CH), 2 * CH)
+            prepare(1, i, n == 0)
+            dki = dk[i] + nn(tb[rows, :], qs[H * QB :, :])
+            dvi = dv[i] + nn(pb[rows, :], gs[H * QB :, :])
+
+            @pl.when(i < NX - 1)
             def _():
-                dqt[b] = dqc
-
-            @pl.when(i > 0)
+                for half in range(2):
+                    rs1_out[i, half, :, :C] = dki[half * CH : (half + 1) * CH].astype(BF16)
+                    rs1_out[i, half, :, C:] = dvi[half * CH : (half + 1) * CH].astype(BF16)
+                for copy in chunk_copies(i):
+                    copy.start()
+
+            @pl.when(i == NX - 1)
             def _():
-                dqt[b] = dqt[b] + dqc
+                dk[i] = dki
+                dv[i] = dvi
 
             return 0
 
@@ -364,16 +382,18 @@
         kt[i] = jnp.concatenate([kv[ra, :C], kv[rb, :C]], axis=0).astype(F32).T.astype(BF16)
     stat_ring(0)
     stat_final(0)
-    second(0, 0, NX // 2)
+    prepare_0()
+    dq_start(0)
+    grads_0(0)
     stat_ring(1)
-    second(0, NX // 2, NX)
-    dq_start(0)
+    grads_0(1)
     stat_final(1)
-    second(1, 0, NX // 2)
+    second_1(0, 2)
     dq_ring(0)
-    second(1, NX // 2, NX)
+    second_1(2, NX)
     dq_start(1)
 
+    dq_ring(1)
     for i in range(NX - 1):
         for copy in chunk_copies(i):
             copy.wait_recv()
@@ -398,7 +418,6 @@
         for copy in rs2_copies(j):
             copy.start()
 
-    dq_ring(1)
     total = dqz_own[...]
     for j in range(1, NZ):
         sender = lax.rem(z + j, NZ)
@@ -455,11 +474,28 @@
         dqf_copy(jz, jc).wait_send()
 
 
+def write_out(a, b, c, a_out, b_out, c_out, sem):
+    copies = [
+        pltpu.make_async_copy(src, dst, sem.at[n])
+        for n, (src, dst) in enumerate(((a, a_out), (b, b_out), (c, c_out)))
+    ]
+    for copy in copies:
+        copy.start()
+    for copy in copies:
+        copy.wait()
+
+
 def shards(queries, keys, values, grad_out, visible, counts):
     vmem = pl.BlockSpec(memory_space=pltpu.VMEM)
     dma = pltpu.SemaphoreType.DMA
     V = pltpu.VMEM
+    blocks = NX * NZH * NY * 2
     scratch = [
+        V((2, blocks), jnp.int32),
+        V((1, blocks), jnp.int32),
+        V((KEYS, H * QB), BF16),
+        V((KEYS, H * QB), BF16),
+        dma((8,)),
         V((KEYS, 2 * C), BF16),
         V((NZH, 2, QB, C), BF16),
         V((NZH, 8, 128), F32),
@@ -495,20 +531,26 @@
     sems = [(NX - 1,)] * 8 + [(1,)] * 6 + [(NZH, NZ - 1)] * 2 + [(NZH,)] * 2 + [(NX - 1,)] * 8
     sems += [(NZH,)] * 2 + [(NZ,)] * 2 + [(NZL * NC - 1,)] * 2
     scratch += [dma(s) for s in sems]
-    return pl.pallas_call(
+    shapes = [(QB, C), (2 * KB, C), (2 * KB, C)]
+    anywhere = pl.BlockSpec(memory_space=pl.ANY)
+    grads = pl.pallas_call(
         kernel,
-        out_shape=(
-            jax.ShapeDtypeStruct((QB, C), BF16),
-            jax.ShapeDtypeStruct((2 * KB, C), BF16),
-            jax.ShapeDtypeStruct((2 * KB, C), BF16),
-        ),
-        in_specs=[vmem] * 6,
+        out_shape=tuple(pltpu.VMEM(s, BF16) for s in shapes),
+        in_specs=[anywhere] * 6,
         out_specs=(vmem,) * 3,
         scratch_shapes=scratch,
         compiler_params=pltpu.CompilerParams(
-            collective_id=0, has_side_effects=True, vmem_limit_bytes=60 * 1024 * 1024
+            collective_id=0, has_side_effects=True, vmem_limit_bytes=62 * 1024 * 1024
         ),
     )(queries, grad_out, keys, values, visible, counts.reshape(1, -1))
+    grads = [pltpu.with_memory_space_constraint(g, pltpu.VMEM) for g in grads]
+    return pl.pallas_call(
+        write_out,
+        out_shape=tuple(jax.ShapeDtypeStruct(s, BF16) for s in shapes),
+        in_specs=[vmem] * 3,
+        out_specs=(anywhere,) * 3,
+        scratch_shapes=[dma((3,))],
+    )(*grads)
 
 
 def solution(mesh):

time: 58.6 us -> 53.7 us (0.916)
  local copies, waits for them, and re-layouts: 2.96 us -> 0 us
  Pallas kernels: 54.4 us -> 52.9 us
    unnamed x7 -> x0, local copies, waits for them, and re-layouts: 2.96 us -> none
    pallas_call x1 -> x2, Pallas kernels: 54.4 us -> 52.9 us  [the longest x1 52.2 us: shards(): pl.pallas_call(kernel, out_shape=tuple((pltpu.VMEM(s, BF16) for s in shap...]
where the time goes in v3:
time: 53.7 us; the launch traced here: 53.5 us
  Pallas kernels  52.9 us (99%)
  between operations  0.64 us (1%)
    pallas_call x1, Pallas kernels, shards(): pl.pallas_call(kernel, out_shape=tuple((pltpu.VMEM(s, BF16) for s in shap...  52.2 us

profile of v3, /device:TPU:1, one launch (start us, length us, event | category | flops | bytes accessed | tf_op | source)
XLA Modules:
  0.0 53.5 jit_solution(6088741090495069970)
XLA Ops:
  0.6 52.2 %shard_map.85 = (bf16[256,256]{1,0:T(8,128)(2,1)S(1)}, bf16[64,256]{1,0:T(8,128)(2,1)S(1)}, bf16[64,256]{1,0:T(8,128)(2,1)S(1)}) custom-call(bf16[256,256]{1,0:T(8,128)(2,1)} %q_in.1, bf16[256,256]{1,0:T(8,128)(2,1)} %g_in.1, bf16[64,256]{1,0:T(8,128)(2,1)} %k_in.1, bf16[64,256]{1,0:T(8,128)(2,1)} %v_in.1, s32[2,64]{1,0:T(2,128)} %vis_in.1, s32[1,64]{1,0:T(1,128)} %bitcast.1), custom_call_target="tpu_custom_call" | custom-call | tf_op jit(solution)/shard_map/pallas_call | solution.py:536
  52.8 0.7 %shard_map.86 = (bf16[256,256]{1,0:T(8,128)(2,1)}, bf16[64,256]{1,0:T(8,128)(2,1)}, bf16[64,256]{1,0:T(8,128)(2,1)}) custom-call(bf16[256,256]{1,0:T(8,128)(2,1)S(1)} %get-tuple-element.6.a, bf16[64,256]{1,0:T(8,128)(2,1)S(1)} %get-tuple-element.7.b, bf16[64,256]{1,0:T(8,128)(2,1)S(1)} %get-tuple-element.8.c), custom_call_target="tpu_custom_call" | custom-call | tf_op jit(solution)/shard_map/pallas_call | solution.py:547

commit v4 on v3

--- a/solution.py
+++ b/solution.py
@@ -55,7 +55,7 @@
     cstat, stat, stat_in, core_out, core_in, alpha, delta,
     dk, dv, rs1_out, rs1_in, rs2_own, rs2_out, rs2_in,
     dqt, dq, dq_sib, dqz_own, dqz_out, dqz_in, dqf_out, dqf_in,
-    ga1_s, ga1_r, gb1_s, gb1_r, ga2_s, ga2_r, gb2_s, gb2_r,
+    ga0_s, ga0_r, gb0_s, gb0_r, ga1_s, ga1_r, gb1_s, gb1_r, ga2_s, ga2_r, gb2_s, gb2_r,
     qx_s, qx_r, qc_s, qc_r, vx_s, vx_r,
     st_s, st_r, sc_s, sc_r,
     ra1_s, ra1_r, rb1_s, rb1_r, ra2_s, ra2_r, rb2_s, rb2_r,
@@ -96,18 +96,18 @@
     for peer in peers:
         pl.semaphore_signal(barrier, inc=1, device_id=peer, device_id_type=pl.DeviceIdType.MESH)
 
-    own_a = pl.multiple_of(y * CH + x * KB, KB)
-    own_b = pl.multiple_of(HALF + x * CH + y * KB, KB)
+    LANES = C // 2
     loads = [
-        (k_in.at[pl.ds(0, KB)], kv.at[pl.ds(own_a, KB), pl.ds(0, C)]),
-        (v_in.at[pl.ds(0, KB)], kv.at[pl.ds(own_a, KB), pl.ds(C, C)]),
-        (k_in.at[pl.ds(KB, KB)], kv.at[pl.ds(own_b, KB), pl.ds(0, C)]),
-        (v_in.at[pl.ds(KB, KB)], kv.at[pl.ds(own_b, KB), pl.ds(C, C)]),
-        (q_in, qd.at[zh, 0]),
-        (g_in, qd.at[zh, 1]),
+        (k_in.at[pl.ds(0, KB)], kv.at[pl.ds(0, KB), pl.ds(0, C)]),
+        (v_in.at[pl.ds(0, KB)], kv.at[pl.ds(0, KB), pl.ds(C, C)]),
+        (k_in.at[pl.ds(KB, KB)], kv.at[pl.ds(CH, KB), pl.ds(0, C)]),
+        (v_in.at[pl.ds(KB, KB)], kv.at[pl.ds(CH, KB), pl.ds(C, C)]),
         (vis_in, vis_i),
         (cnt_in, cnt),
     ]
+    for part in range(2):
+        lanes = pl.ds(part * LANES, LANES)
+        loads += [(q_in.at[:, lanes], qd.at[zh, part, 0]), (g_in.at[:, lanes], qd.at[zh, part, 1])]
     loads = [pltpu.make_async_copy(src, dst, in_s.at[n]) for n, (src, dst) in enumerate(loads)]
     for copy in loads:
         copy.start()
@@ -117,40 +117,57 @@
 
     pl.semaphore_wait(barrier, len(peers))
 
-    ga1 = [remote(kv.at[pl.ds(own_a, KB)], kv.at[pl.ds(own_a, KB)], ga1_s.at[j - 1], ga1_r.at[j - 1], xp(j)) for j in range(1, NX)]
-    gb1 = [remote(kv.at[pl.ds(own_b, KB)], kv.at[pl.ds(own_b, KB)], gb1_s.at[j - 1], gb1_r.at[j - 1], yp(j)) for j in range(1, NY)]
+    def rows_to(src, dst, count, sems, j, device):
+        return remote(kv.at[pl.ds(src, count)], kv.at[pl.ds(dst, count)], sems[0].at[j - 1], sems[1].at[j - 1], device)
+
+    js = range(1, NX)
+    ga1 = [rows_to(0, (NX - j) * KB, KB, (ga1_s, ga1_r), j, xp(j)) for j in js]
+    gb1 = [rows_to(CH, CH + (NY - j) * KB, KB, (gb1_s, gb1_r), j, yp(j)) for j in js]
+    place = {0: 0, 1: 1, NX - 1: 2, 2: 3}
+    ga0 = [rows_to(0, place[NY - j] * 2 * CH, KB, (ga0_s, ga0_r), j, yp(j)) for j in js]
+    gb0 = [rows_to(CH, place[NX - j] * 2 * CH + CH, KB, (gb0_s, gb0_r), j, xp(j)) for j in js]
+    ga2 = [rows_to(KB, place[NY - j] * 2 * CH + KB, CH - KB, (ga2_s, ga2_r), j, yp(j)) for j in js]
+    gb2 = [rows_to(CH + KB, place[NX - j] * 2 * CH + CH + KB, CH - KB, (gb2_s, gb2_r), j, xp(j)) for j in js]
+    qx = [remote(qd.at[zh, part, core], qd.at[zh, part, core], qx_s.at[part], qx_r.at[part], mirror) for part in range(2)]
+    qc = [remote(qd.at[1 - zh, part, core], qd.at[1 - zh, part, core], qc_s.at[part], qc_r.at[part], sibling) for part in range(2)]
     for copy in ga1 + gb1:
         copy.start()
-    qx = remote(qd.at[zh, core], qd.at[zh, core], qx_s.at[0], qx_r.at[0], mirror)
-    qx.start()
+    qx[0].start()
+    qx[1].start()
     vx = remote(vis.at[zh], vis.at[zh], vx_s.at[0], vx_r.at[0], zp(NZL))
     vx.start()
-
-    head_of = lax.broadcasted_iota(jnp.int32, (QB, C), 1) // HD
-
-    def stack(b):
-        qb = qd[b, 0]
-        gb = qd[b, 1]
+    for copy in ga0 + gb0:
+        copy.start()
+
+    head_of = lax.broadcasted_iota(jnp.int32, (QB, LANES), 1) // HD
+
+    def stack(b, part):
+        qb = qd[b, part, 0]
+        gb = qd[b, part, 1]
+        zero = jnp.zeros_like(qb)
 
         def one(h, _):
-            row = pl.multiple_of((b * H + h) * QB, QB)
+            rows = pl.ds(pl.multiple_of((b * H + part * (H // 2) + h) * QB, QB), QB)
             keep = head_of == h
-            qs[pl.ds(row, QB), :] = jnp.where(keep, qb, jnp.zeros_like(qb))
-            gs[pl.ds(row, QB), :] = jnp.where(keep, gb, jnp.zeros_like(gb))
+            for ref, block in ((qs, qb), (gs, gb)):
+                ref[rows, part * LANES : (part + 1) * LANES] = jnp.where(keep, block, zero)
+                ref[rows, (1 - part) * LANES : (2 - part) * LANES] = zero
             return 0
 
-        lax.fori_loop(0, H, one, 0)
-
-    stack(zh)
+        lax.fori_loop(0, H // 2, one, 0)
+
+    stack(zh, 0)
+    stack(zh, 1)
 
     blocks = NX * NZH * NY * 2
     row = lax.broadcasted_iota(jnp.int32, (KEYS, blocks), 0)
     col = lax.broadcasted_iota(jnp.int32, (KEYS, blocks), 1)
-    half = row // HALF
-    outer = (row % HALF) // CH
+    half = (row % (2 * CH)) // CH
+    outer = row // (2 * CH)
+    outer = jnp.where(outer == 3, 2, jnp.where(outer == 2, 3, outer))
     inner = (row % CH) // KB
-    bx = jnp.where(half == 0, inner, outer)
-    by = jnp.where(half == 0, outer, inner)
+    bx = (x + jnp.where(half == 0, inner, outer)) % NX
+    by = (y + jnp.where(half == 0, outer, inner)) % NY
     block = 2 * ((bx * NZH + zh) * NY + by) + half
     pick = ((block == col) & (row % KB < cnt[...])).astype(F32).astype(BF16)
 
@@ -162,44 +179,39 @@
 
     cap_of(zh)
 
-    chunk_a = pl.multiple_of(y * CH, CH)
-    chunk_b = pl.multiple_of(HALF + x * CH, CH)
-    for copy in ga1 + gb1:
-        copy.wait_recv()
-    ga2 = [remote(kv.at[pl.ds(chunk_a, CH)], kv.at[pl.ds(chunk_a, CH)], ga2_s.at[j - 1], ga2_r.at[j - 1], yp(j)) for j in range(1, NY)]
-    gb2 = [remote(kv.at[pl.ds(chunk_b, CH)], kv.at[pl.ds(chunk_b, CH)], gb2_s.at[j - 1], gb2_r.at[j - 1], xp(j)) for j in range(1, NX)]
-    for j in (0, 2, 1):
-        ga2[j].start()
-        gb2[j].start()
-
-    def chunk_rows(i):
-        ra = pl.ds(pl.multiple_of(lax.rem(y + 1 + i, NY) * CH, CH), CH)
-        rb = pl.ds(pl.multiple_of(HALF + lax.rem(x + 1 + i, NX) * CH, CH), CH)
-        return ra, rb
-
-    def first(b, i):
-        ra, rb = chunk_rows(i)
-        kc = jnp.concatenate([kv[ra, :C], kv[rb, :C]], axis=0)
-        vc = jnp.concatenate([kv[ra, C:], kv[rb, C:]], axis=0)
-        n = b * NX + i
-        for h in range(H):
+    for one_stage, next_stage in ((ga1, ga2), (gb1, gb2)):
+        for copy in one_stage:
+            copy.wait_recv()
+        for j in (0, 2, 1):
+            next_stage[j].start()
+
+    def chunk_rows(i, count=1):
+        return pl.ds(i * 2 * CH, count * 2 * CH)
+
+    def first(b, i, count, heads):
+        rk = chunk_rows(i, count)
+        kc = kv[rk, :C]
+        vc = kv[rk, C:]
+        for h in heads:
             rows = pl.ds(pl.multiple_of((b * H + h) * QB, QB), QB)
             s = nt(kc, qs[rows, :]) * (SCALE * LOG2E)
-            s = jnp.minimum(s, jnp.concatenate([cap[b, ra, :], cap[b, rb, :]], axis=0))
+            s = jnp.minimum(s, cap[b, rk, :])
             m = jnp.maximum(jnp.max(s, axis=0, keepdims=True), 0.1 * NEG)
             p = jnp.exp2(s - m)
-            pbuf[n, h] = p
             d = nt(vc, gs[rows, :])
-            dbuf[n, h] = d
-            cstat[n, 0, h : h + 1, :] = m
-            cstat[n, 1, h : h + 1, :] = jnp.sum(p, axis=0, keepdims=True)
-            cstat[n, 2, h : h + 1, :] = jnp.sum(p * d, axis=0, keepdims=True)
+            for u in range(count):
+                pbuf[b * NX + i + u, h] = p[u * 2 * CH : (u + 1) * 2 * CH]
+                dbuf[b * NX + i + u, h] = d[u * 2 * CH : (u + 1) * 2 * CH]
+            group = b * 3 + min(i, 1) + (i == 3)
+            cstat[group, 0, h : h + 1, :] = m
+            cstat[group, 1, h : h + 1, :] = jnp.sum(p, axis=0, keepdims=True)
+            cstat[group, 2, h : h + 1, :] = jnp.sum(p * d, axis=0, keepdims=True)
 
     def stat_copies(b):
         return [remote(stat.at[b], stat_in.at[b, j - 1], st_s.at[b, j - 1], st_r.at[b, j - 1], zp(j)) for j in range(1, NZ)]
 
     def stat_send(b):
-        parts = [tuple(cstat[b * NX + i, k] for k in range(3)) for i in range(NX)]
+        parts = [tuple(cstat[b * 3 + i, k] for k in range(3)) for i in range(3)]
         top = parts[0][0]
         for part in parts[1:]:
             top = jnp.maximum(top, part[0])
@@ -212,8 +224,9 @@
         total = jnp.maximum(total, 1e-30)
         stat[b, 0] = top + jnp.log2(total)
         stat[b, 1] = dot / total
-        for copy in stat_copies(b):
-            copy.start()
+        copies = stat_copies(b)
+        for j in (4, 3, 5, 2, 6, 1, 7):
+            copies[j - 1].start()
 
     def core_copy(b):
         return remote(core_out.at[b], core_in.at[b], sc_s.at[b], sc_r.at[b], sibling)
@@ -242,22 +255,24 @@
     def stat_final(b):
         core_copy(b).wait_recv()
         lse, mean = merge([(core_out[b, 0], core_out[b, 1]), (core_in[b, 0], core_in[b, 1])])
-        for i in range(NX):
-            alpha[b * NX + i] = jnp.exp2(cstat[b * NX + i, 0] - lse)
+        for i in range(3):
+            alpha[b * 3 + i] = jnp.exp2(cstat[b * 3 + i, 0] - lse)
         delta[b] = mean
 
     def chunk_copies(i):
+        r = jnp.where(i == 3, 2, jnp.where(i == 2, 3, 1))
         return (
-            remote(rs1_out.at[i, 0], rs1_in.at[i, 0], ra1_s.at[i], ra1_r.at[i], yp(i + 1)),
-            remote(rs1_out.at[i, 1], rs1_in.at[i, 1], rb1_s.at[i], rb1_r.at[i], xp(i + 1)),
+            remote(rs1_out.at[i - 1, 0], rs1_in.at[r - 1, 0], ra1_s.at[r - 1], ra1_r.at[r - 1], yp(r)),
+            remote(rs1_out.at[i - 1, 1], rs1_in.at[r - 1, 1], rb1_s.at[r - 1], rb1_r.at[r - 1], xp(r)),
         )
 
     def prepare(b, i, first_chunk):
         n = b * NX + i
+        group = b * 3 + jnp.where(i == 0, 0, jnp.where(i == 3, 2, 1))
         rows = pl.ds(pl.multiple_of(i * 2 * CH, 2 * CH), 2 * CH)
         dqs = []
         for h in range(H):
-            a = alpha[n, h : h + 1, :]
+            a = alpha[group, h : h + 1, :]
             e = delta[b, h : h + 1, :]
             p = pbuf[n, h] * a
             t = (p * (dbuf[n, h] - e)).astype(BF16)
@@ -291,21 +306,21 @@
 
     def second_1(lo, hi):
         def one(n, _):
-            i = jnp.where(n < 2, 1 - n, n)
+            i = jnp.where(n == 0, 3, jnp.where(n == 3, 0, n))
             rows = pl.ds(pl.multiple_of(i * 2 * CH, 2 * CH), 2 * CH)
             prepare(1, i, n == 0)
             dki = dk[i] + nn(tb[rows, :], qs[H * QB :, :])
             dvi = dv[i] + nn(pb[rows, :], gs[H * QB :, :])
 
-            @pl.when(i < NX - 1)
+            @pl.when(i > 0)
             def _():
                 for half in range(2):
-                    rs1_out[i, half, :, :C] = dki[half * CH : (half + 1) * CH].astype(BF16)
-                    rs1_out[i, half, :, C:] = dvi[half * CH : (half + 1) * CH].astype(BF16)
+                    rs1_out[i - 1, half, :, :C] = dki[half * CH : (half + 1) * CH].astype(BF16)
+                    rs1_out[i - 1, half, :, C:] = dvi[half * CH : (half + 1) * CH].astype(BF16)
                 for copy in chunk_copies(i):
                     copy.start()
 
-            @pl.when(i == NX - 1)
+            @pl.when(i == 0)
             def _():
                 dk[i] = dki
                 dv[i] = dvi
@@ -346,40 +361,40 @@
             def _(j=j):
                 dq_slot(b, j).start()
 
-    first(zh, NX - 1)
+    head_parts = (range(H // 2), range(H // 2, H))
+    first(zh, 0, 1, range(H))
     vx.wait_recv()
     cap_of(1 - zh)
-    qx.wait_recv()
-    qc = remote(qd.at[1 - zh, core], qd.at[1 - zh, core], qc_s.at[0], qc_r.at[0], sibling)
-    qc.start()
-    qc.wait_recv()
-    stack(1 - zh)
-
-    def unit(n, _):
-        for step, j in enumerate((2, 0, 1)):
-
-            @pl.when(n == step)
-            def _(j=j):
-                ga2[j].wait_recv()
-                gb2[j].wait_recv()
-
-        in_0 = NX - 1 + zh
-        b = (n >= in_0).astype(jnp.int32)
-        place = jnp.where(b == 0, n + 1 - zh, n - in_0 + zh)
-        i = jnp.where(place == 0, NX - 1, jnp.where(place == 1, 0, jnp.where(place == 2, 2, 1)))
-        first(b, i)
-
-        @pl.when(n == in_0 - 1)
+    for part, heads in enumerate(head_parts):
+        qx[part].wait_recv()
+        qc[part].start()
+        qc[part].wait_recv()
+        stack(1 - zh, part)
+        first(1 - zh, 0, 1, heads)
+
+    def shard(b, _):
+        @pl.when(b == 0)
         def _():
-            stat_send(0)
-
+            for j in (0, 2):
+                for copies in (ga0, gb0, ga2, gb2):
+                    copies[j].wait_recv()
+
+        first(b, 1, 2, range(H))
+
+        @pl.when(b == 0)
+        def _():
+            for copies in (ga0, gb0, ga2, gb2):
+                copies[1].wait_recv()
+
+        first(b, 3, 1, range(H))
+        stat_send(b)
         return 0
 
-    lax.fori_loop(0, NZH * NX - 1, unit, 0)
-    stat_send(1)
+    lax.fori_loop(0, NZH, shard, 0)
     for i in range(NX):
-        ra, rb = chunk_rows(i)
-        kt[i] = jnp.concatenate([kv[ra, :C], kv[rb, :C]], axis=0).astype(F32).T.astype(BF16)
+        kt[i] = kv[i * 2 * CH : (i + 1) * 2 * CH, :C].astype(F32).T.astype(BF16)
+    for copy in ga0 + gb0 + ga1 + gb1 + ga2 + gb2 + qx + qc + [vx]:
+        copy.wait_send()
     stat_ring(0)
     stat_final(0)
     prepare_0()
@@ -394,29 +409,25 @@
     dq_start(1)
 
     dq_ring(1)
-    for i in range(NX - 1):
-        for copy in chunk_copies(i):
-            copy.wait_recv()
+    def rs2_copies(j):
+        rows = pl.ds(j * KB, KB)
+        return (
+            remote(rs2_out.at[0, rows], rs2_in.at[j - 1, 0], ra2_s.at[j - 1], ra2_r.at[j - 1], xp(j)),
+            remote(rs2_out.at[1, rows], rs2_in.at[j - 1, 1], rb2_s.at[j - 1], rb2_r.at[j - 1], yp(j)),
+        )
+
     for half in range(2):
+        for r in js:
+            chunk_copies(r)[half].wait_recv()
         for part, acc in enumerate((dk, dv)):
             cols = slice(part * C, (part + 1) * C)
-            total = acc[NX - 1, half * CH : (half + 1) * CH, :]
+            total = acc[0, half * CH : (half + 1) * CH, :]
             for i in range(NX - 1):
                 total = total + rs1_in[i, half, :, cols].astype(F32)
-            rs2_own[half, :, cols] = total
+            rs2_own[half, :, cols] = total[:KB]
             rs2_out[half, :, cols] = total.astype(BF16)
-
-    def rs2_copies(j):
-        rows_a = pl.ds(pl.multiple_of(lax.rem(x + j, NX) * KB, KB), KB)
-        rows_b = pl.ds(pl.multiple_of(lax.rem(y + j, NY) * KB, KB), KB)
-        return (
-            remote(rs2_out.at[0, rows_a], rs2_in.at[j - 1, 0], ra2_s.at[j - 1], ra2_r.at[j - 1], xp(j)),
-            remote(rs2_out.at[1, rows_b], rs2_in.at[j - 1, 1], rb2_s.at[j - 1], rb2_r.at[j - 1], yp(j)),
-        )
-
-    for j in range(1, NX):
-        for copy in rs2_copies(j):
-            copy.start()
+        for j in (2, 1, 3):
+            rs2_copies(j)[half].start()
 
     total = dqz_own[...]
     for j in range(1, NZ):
@@ -434,25 +445,6 @@
         dqf_copy(jz, jc).start()
     gq_out[pl.ds(pl.multiple_of(core * QH + zl * QS, QS), QS), :] = dqf_out[...]
 
-    for j in range(1, NX):
-        for copy in rs2_copies(j):
-            copy.wait_recv()
-    for half, pos in ((0, x), (1, y)):
-        rows = pl.ds(pl.multiple_of(pos * KB, KB), KB)
-        total = rs2_own[half, rows, :]
-        for j in range(NX - 1):
-            total = total + rs2_in[j, half].astype(F32)
-        gk_out[half * KB : (half + 1) * KB, :] = (total[:, :C] * SCALE).astype(BF16)
-        gv_out[half * KB : (half + 1) * KB, :] = total[:, C:].astype(BF16)
-
-    for jz, jc in others:
-        dqf_copy(jz, jc).wait_recv()
-        fz = lax.rem(zl - jz + NZL, NZL)
-        fc = lax.rem(core - jc + NC, NC)
-        gq_out[pl.ds(pl.multiple_of(fc * QH + fz * QS, QS), QS), :] = dqf_in[jz * NC + jc - 1]
-
-    for copy in ga1 + gb1 + ga2 + gb2 + [qx, vx, qc]:
-        copy.wait_send()
     for b in range(NZH):
         for copy in stat_copies(b):
             copy.wait_send()
@@ -464,10 +456,26 @@
             def _(b=b, j=j):
                 dq_slot(b, j).wait_send()
 
-    for i in range(NX - 1):
-        for copy in chunk_copies(i):
+    for r in js:
+        for copy in chunk_copies(r):
             copy.wait_send()
     for j in range(1, NX):
+        for copy in rs2_copies(j):
+            copy.wait_recv()
+    for half in range(2):
+        total = rs2_own[half]
+        for j in range(NX - 1):
+            total = total + rs2_in[j, half].astype(F32)
+        gk_out[half * KB : (half + 1) * KB, :] = (total[:, :C] * SCALE).astype(BF16)
+        gv_out[half * KB : (half + 1) * KB, :] = total[:, C:].astype(BF16)
+
+    for jz, jc in others:
+        dqf_copy(jz, jc).wait_recv()
+        fz = lax.rem(zl - jz + NZL, NZL)
+        fc = lax.rem(core - jc + NC, NC)
+        gq_out[pl.ds(pl.multiple_of(fc * QH + fz * QS, QS), QS), :] = dqf_in[jz * NC + jc - 1]
+
+    for j in js:
         for copy in rs2_copies(j):
             copy.wait_send()
     for jz, jc in others:
@@ -495,9 +503,9 @@
         V((1, blocks), jnp.int32),
         V((KEYS, H * QB), BF16),
         V((KEYS, H * QB), BF16),
-        dma((8,)),
+        dma((10,)),
         V((KEYS, 2 * C), BF16),
-        V((NZH, 2, QB, C), BF16),
+        V((NZH, 2, 2, QB, C // 2), BF16),
         V((NZH, 8, 128), F32),
         V((NZH * H * QB, C), BF16),
         V((NZH * H * QB, C), BF16),
@@ -505,18 +513,18 @@
         V((NZH * NX, H, 2 * CH, QB), F32),
         V((NZH, KEYS, QB), F32),
         V((NX, C, 2 * CH), BF16),
-        V((NZH * NX, 3, H, QB), F32),
+        V((NZH * 3, 3, H, QB), F32),
         V((NZH, 2, H, QB), F32),
         V((NZH, NZ - 1, 2, H, QB), F32),
         V((NZH, 2, H, QB), F32),
         V((NZH, 2, H, QB), F32),
-        V((NZH * NX, H, QB), F32),
+        V((NZH * 3, H, QB), F32),
         V((NZH, H, QB), F32),
         V((NX, 2 * CH, C), F32),
         V((NX, 2 * CH, C), F32),
         V((NX - 1, 2, CH, 2 * C), BF16),
         V((NX - 1, 2, CH, 2 * C), BF16),
-        V((2, CH, 2 * C), F32),
+        V((2, KB, 2 * C), F32),
         V((2, CH, 2 * C), BF16),
         V((NX - 1, 2, KB, 2 * C), BF16),
         V((NZH, C, QB), F32),
@@ -528,7 +536,7 @@
         V((QS, C), BF16),
         V((NZL * NC - 1, QS, C), BF16),
     ]
-    sems = [(NX - 1,)] * 8 + [(1,)] * 6 + [(NZH, NZ - 1)] * 2 + [(NZH,)] * 2 + [(NX - 1,)] * 8
+    sems = [(NX - 1,)] * 12 + [(2,)] * 6 + [(NZH, NZ - 1)] * 2 + [(NZH,)] * 2 + [(NX - 1,)] * 8
     sems += [(NZH,)] * 2 + [(NZ,)] * 2 + [(NZL * NC - 1,)] * 2
     scratch += [dma(s) for s in sems]
     shapes = [(QB, C), (2 * KB, C), (2 * KB, C)]

time: 53.7 us -> 52.2 us (0.972)
  Pallas kernels: 52.9 us -> 51.4 us
    pallas_call x1, Pallas kernels: 52.2 us -> 50.7 us  [shards(): pl.pallas_call(kernel, out_shape=tuple((pltpu.VMEM(s, BF16) for s in shap...]
where the time goes in v4:
time: 52.2 us; the launch traced here: 52.1 us
  Pallas kernels  51.4 us (98%)
  between operations  0.64 us (1%)
    pallas_call x1, Pallas kernels, shards(): pl.pallas_call(kernel, out_shape=tuple((pltpu.VMEM(s, BF16) for s in shap...  50.7 us

profile of v4, /device:TPU:1, one launch (start us, length us, event | category | flops | bytes accessed | tf_op | source)
XLA Modules:
  0.0 52.1 jit_solution(10287440038234571059)
XLA Ops:
  0.6 50.7 %shard_map.85 = (bf16[256,256]{1,0:T(8,128)(2,1)S(1)}, bf16[64,256]{1,0:T(8,128)(2,1)S(1)}, bf16[64,256]{1,0:T(8,128)(2,1)S(1)}) custom-call(bf16[256,256]{1,0:T(8,128)(2,1)} %q_in.1, bf16[256,256]{1,0:T(8,128)(2,1)} %g_in.1, bf16[64,256]{1,0:T(8,128)(2,1)} %k_in.1, bf16[64,256]{1,0:T(8,128)(2,1)} %v_in.1, s32[2,64]{1,0:T(2,128)} %vis_in.1, s32[1,64]{1,0:T(1,128)} %bitcast.1), custom_call_target="tpu_custom_call" | custom-call | tf_op jit(solution)/shard_map/pallas_call | solution.py:544
  51.4 0.7 %shard_map.86 = (bf16[256,256]{1,0:T(8,128)(2,1)}, bf16[64,256]{1,0:T(8,128)(2,1)}, bf16[64,256]{1,0:T(8,128)(2,1)}) custom-call(bf16[256,256]{1,0:T(8,128)(2,1)S(1)} %get-tuple-element.6.a, bf16[64,256]{1,0:T(8,128)(2,1)S(1)} %get-tuple-element.7.b, bf16[64,256]{1,0:T(8,128)(2,1)S(1)} %get-tuple-element.8.c), custom_call_target="tpu_custom_call" | custom-call | tf_op jit(solution)/shard_map/pallas_call | solution.py:555

commit v5 on v4

--- a/solution.py
+++ b/solution.py
@@ -51,7 +51,7 @@
 def kernel(
     q_in, g_in, k_in, v_in, vis_in, cnt_in,
     gq_out, gk_out, gv_out,
-    vis_i, cnt, pb, tb, in_s, kv, qd, vis, qs, gs, pbuf, dbuf, cap, kt,
+    vis_i, cnt, pb_0, pb_1, tb_0, tb_1, in_s, kv, qd, vis, qs, gs, pbuf, dbuf, cap, kt,
     cstat, stat, stat_in, core_out, core_in, alpha, delta,
     dk, dv, rs1_out, rs1_in, rs2_own, rs2_out, rs2_in,
     dqt, dq, dq_sib, dqz_own, dqz_out, dqz_in, dqf_out, dqf_in,
@@ -61,6 +61,8 @@
     ra1_s, ra1_r, rb1_s, rb1_r, ra2_s, ra2_r, rb2_s, rb2_r,
     dc_s, dc_r, dz_s, dz_r, df_s, df_r,
 ):
+    pb = (pb_0, pb_1)
+    tb = (tb_0, tb_1)
     cam = lax.axis_index("cam")
     tile = lax.axis_index("tile")
     core = lax.rem(cam, NC)
@@ -91,8 +93,8 @@
     mirror = at(x, y, NZ - 1 - z, core)
 
     barrier = pltpu.get_barrier_semaphore()
-    peers = [xp(j) for j in range(1, NX)] + [yp(j) for j in range(1, NY)] + [zp(j) for j in range(1, NZ)]
-    peers += [fp(jz, 1) for jz in range(NZL)]
+    peers = [zp(j) for j in (4, 3, 5, 2, 6, 1, 7)] + [fp(jz, 1) for jz in (3, 2, 1, 0)]
+    peers += [yp(j) for j in range(1, NY)] + [xp(j) for j in range(1, NX)]
     for peer in peers:
         pl.semaphore_signal(barrier, inc=1, device_id=peer, device_id_type=pl.DeviceIdType.MESH)
 
@@ -260,74 +262,43 @@
         delta[b] = mean
 
     def chunk_copies(i):
-        r = jnp.where(i == 3, 2, jnp.where(i == 2, 3, 1))
+        r = {1: 1, 2: NX - 1, 3: 2}[i]
         return (
             remote(rs1_out.at[i - 1, 0], rs1_in.at[r - 1, 0], ra1_s.at[r - 1], ra1_r.at[r - 1], yp(r)),
             remote(rs1_out.at[i - 1, 1], rs1_in.at[r - 1, 1], rb1_s.at[r - 1], rb1_r.at[r - 1], xp(r)),
         )
 
-    def prepare(b, i, first_chunk):
+    def prepare(b, i, slot, first_chunk):
         n = b * NX + i
-        group = b * 3 + jnp.where(i == 0, 0, jnp.where(i == 3, 2, 1))
-        rows = pl.ds(pl.multiple_of(i * 2 * CH, 2 * CH), 2 * CH)
+        group = b * 3 + min(i, 1) + (i == 3)
         dqs = []
         for h in range(H):
             a = alpha[group, h : h + 1, :]
             e = delta[b, h : h + 1, :]
             p = pbuf[n, h] * a
             t = (p * (dbuf[n, h] - e)).astype(BF16)
-            pb[rows, h * QB : (h + 1) * QB] = p.astype(BF16)
-            tb[rows, h * QB : (h + 1) * QB] = t
+            pb[slot][:, h * QB : (h + 1) * QB] = p.astype(BF16)
+            tb[slot][:, h * QB : (h + 1) * QB] = t
             dqs.append(nn(kt[i, h * HD : (h + 1) * HD, :], t))
         dqc = jnp.concatenate(dqs, axis=0)
-
-        @pl.when(first_chunk)
-        def _():
-            dqt[b] = dqc
-
-        @pl.when(jnp.logical_not(first_chunk))
-        def _():
-            dqt[b] = dqt[b] + dqc
-
-    def prepare_0():
-        def one(i, _):
-            prepare(0, i, i == 0)
-            return 0
-
-        lax.fori_loop(0, NX, one, 0)
-
-    def grads_0(pair):
-        rows = slice(pair * 4 * CH, (pair + 1) * 4 * CH)
-        dkc = nn(tb[rows, :], qs[: H * QB, :])
-        dvc = nn(pb[rows, :], gs[: H * QB, :])
-        for u in range(2):
-            dk[2 * pair + u] = dkc[u * 2 * CH : (u + 1) * 2 * CH]
-            dv[2 * pair + u] = dvc[u * 2 * CH : (u + 1) * 2 * CH]
-
-    def second_1(lo, hi):
-        def one(n, _):
-            i = jnp.where(n == 0, 3, jnp.where(n == 3, 0, n))
-            rows = pl.ds(pl.multiple_of(i * 2 * CH, 2 * CH), 2 * CH)
-            prepare(1, i, n == 0)
-            dki = dk[i] + nn(tb[rows, :], qs[H * QB :, :])
-            dvi = dv[i] + nn(pb[rows, :], gs[H * QB :, :])
-
-            @pl.when(i > 0)
-            def _():
-                for half in range(2):
-                    rs1_out[i - 1, half, :, :C] = dki[half * CH : (half + 1) * CH].astype(BF16)
-                    rs1_out[i - 1, half, :, C:] = dvi[half * CH : (half + 1) * CH].astype(BF16)
-                for copy in chunk_copies(i):
-                    copy.start()
-
-            @pl.when(i == 0)
-            def _():
-                dk[i] = dki
-                dv[i] = dvi
-
-            return 0
-
-        lax.fori_loop(lo, hi, one, 0)
+        dqt[b] = dqc if first_chunk else dqt[b] + dqc
+
+    def grads(b, i, slot):
+        stack_rows = slice(b * H * QB, (b + 1) * H * QB)
+        dki = nn(tb[slot][...], qs[stack_rows, :])
+        dvi = nn(pb[slot][...], gs[stack_rows, :])
+        if b == 1:
+            dki = dk[i] + dki
+            dvi = dv[i] + dvi
+        if b == 0 or i == 0:
+            dk[i] = dki
+            dv[i] = dvi
+            return
+        for half in range(2):
+            rs1_out[i - 1, half, :, :C] = dki[half * CH : (half + 1) * CH].astype(BF16)
+            rs1_out[i - 1, half, :, C:] = dvi[half * CH : (half + 1) * CH].astype(BF16)
+        for copy in chunk_copies(i):
+            copy.start()
 
     other_half = pl.ds(pl.multiple_of((1 - core) * QH, QH), QH)
 
@@ -397,16 +368,22 @@
         copy.wait_send()
     stat_ring(0)
     stat_final(0)
-    prepare_0()
-    dq_start(0)
-    grads_0(0)
-    stat_ring(1)
-    grads_0(1)
-    stat_final(1)
-    second_1(0, 2)
-    dq_ring(0)
-    second_1(2, NX)
-    dq_start(1)
+    steps = [(b, i) for b in range(NZH) for i in (3, 1, 2, 0)]
+    prepare(*steps[0], 0, True)
+    for k, step in enumerate(steps):
+        if k == 2:
+            stat_ring(1)
+        if k == 3:
+            stat_final(1)
+        if k + 1 < len(steps):
+            prepare(*steps[k + 1], (k + 1) % 2, steps[k + 1][1] == 3)
+        grads(*step, k % 2)
+        if k == 2:
+            dq_start(0)
+        if k == 4:
+            dq_ring(0)
+        if k == 6:
+            dq_start(1)
 
     dq_ring(1)
     def rs2_copies(j):
@@ -501,8 +478,10 @@
     scratch = [
         V((2, blocks), jnp.int32),
         V((1, blocks), jnp.int32),
-        V((KEYS, H * QB), BF16),
-        V((KEYS, H * QB), BF16),
+        V((2 * CH, H * QB), BF16),
+        V((2 * CH, H * QB), BF16),
+        V((2 * CH, H * QB), BF16),
+        V((2 * CH, H * QB), BF16),
         dma((10,)),
         V((KEYS, 2 * C), BF16),
         V((NZH, 2, 2, QB, C // 2), BF16),

time: 52.2 us -> 51.6 us (0.989)
  Pallas kernels: 51.4 us -> 50.6 us
    pallas_call x1, Pallas kernels: 50.7 us -> 49.9 us  [shards(): pl.pallas_call(kernel, out_shape=tuple((pltpu.VMEM(s, BF16) for s in shap...]
where the time goes in v5:
time: 51.6 us; the launch traced here: 51.4 us
  Pallas kernels  50.6 us (98%)
  between operations  0.8 us (2%)
    pallas_call x1, Pallas kernels, shards(): pl.pallas_call(kernel, out_shape=tuple((pltpu.VMEM(s, BF16) for s in shap...  49.9 us

profile of v5, /device:TPU:1, one launch (start us, length us, event | category | flops | bytes accessed | tf_op | source)
XLA Modules:
  0.0 51.4 jit_solution(12322837518090105632)
XLA Ops:
  0.6 49.9 %shard_map.85 = (bf16[256,256]{1,0:T(8,128)(2,1)S(1)}, bf16[64,256]{1,0:T(8,128)(2,1)S(1)}, bf16[64,256]{1,0:T(8,128)(2,1)S(1)}) custom-call(bf16[256,256]{1,0:T(8,128)(2,1)} %q_in.1, bf16[256,256]{1,0:T(8,128)(2,1)} %g_in.1, bf16[64,256]{1,0:T(8,128)(2,1)} %k_in.1, bf16[64,256]{1,0:T(8,128)(2,1)} %v_in.1, s32[2,64]{1,0:T(2,128)} %vis_in.1, s32[1,64]{1,0:T(1,128)} %bitcast.1), custom_call_target="tpu_custom_call" | custom-call | tf_op jit(solution)/shard_map/pallas_call | solution.py:523
  50.5 0.7 %shard_map.86 = (bf16[256,256]{1,0:T(8,128)(2,1)}, bf16[64,256]{1,0:T(8,128)(2,1)}, bf16[64,256]{1,0:T(8,128)(2,1)}) custom-call(bf16[256,256]{1,0:T(8,128)(2,1)S(1)} %get-tuple-element.6.a, bf16[64,256]{1,0:T(8,128)(2,1)S(1)} %get-tuple-element.7.b, bf16[64,256]{1,0:T(8,128)(2,1)S(1)} %get-tuple-element.8.c), custom_call_target="tpu_custom_call" | custom-call | tf_op jit(solution)/shard_map/pallas_call | solution.py:534

commit v6 on v5

--- a/solution.py
+++ b/solution.py
@@ -334,14 +334,18 @@
 
     head_parts = (range(H // 2), range(H // 2, H))
     first(zh, 0, 1, range(H))
+    qx[0].wait_recv()
+    qc[0].start()
     vx.wait_recv()
     cap_of(1 - zh)
-    for part, heads in enumerate(head_parts):
-        qx[part].wait_recv()
-        qc[part].start()
-        qc[part].wait_recv()
-        stack(1 - zh, part)
-        first(1 - zh, 0, 1, heads)
+    qc[0].wait_recv()
+    stack(1 - zh, 0)
+    qx[1].wait_recv()
+    qc[1].start()
+    first(1 - zh, 0, 1, head_parts[0])
+    qc[1].wait_recv()
+    stack(1 - zh, 1)
+    first(1 - zh, 0, 1, head_parts[1])
 
     def shard(b, _):
         @pl.when(b == 0)

time: 51.6 us -> 51 us (0.988)
    pallas_call x1, Pallas kernels: 49.9 us -> 49.4 us  [shards(): pl.pallas_call(kernel, out_shape=tuple((pltpu.VMEM(s, BF16) for s in shap...]
where the time goes in v6:
time: 51 us; the launch traced here: 50.9 us
  Pallas kernels  50.1 us (98%)
  between operations  0.8 us (2%)
    pallas_call x1, Pallas kernels, shards(): pl.pallas_call(kernel, out_shape=tuple((pltpu.VMEM(s, BF16) for s in shap...  49.4 us

profile of v6, /device:TPU:1, one launch (start us, length us, event | category | flops | bytes accessed | tf_op | source)
XLA Modules:
  0.0 50.9 jit_solution(982762046620129423)
XLA Ops:
  0.6 49.4 %shard_map.85 = (bf16[256,256]{1,0:T(8,128)(2,1)S(1)}, bf16[64,256]{1,0:T(8,128)(2,1)S(1)}, bf16[64,256]{1,0:T(8,128)(2,1)S(1)}) custom-call(bf16[256,256]{1,0:T(8,128)(2,1)} %q_in.1, bf16[256,256]{1,0:T(8,128)(2,1)} %g_in.1, bf16[64,256]{1,0:T(8,128)(2,1)} %k_in.1, bf16[64,256]{1,0:T(8,128)(2,1)} %v_in.1, s32[2,64]{1,0:T(2,128)} %vis_in.1, s32[1,64]{1,0:T(1,128)} %bitcast.1), custom_call_target="tpu_custom_call" | custom-call | tf_op jit(solution)/shard_map/pallas_call | solution.py:527
  50.0 0.7 %shard_map.86 = (bf16[256,256]{1,0:T(8,128)(2,1)}, bf16[64,256]{1,0:T(8,128)(2,1)}, bf16[64,256]{1,0:T(8,128)(2,1)}) custom-call(bf16[256,256]{1,0:T(8,128)(2,1)S(1)} %get-tuple-element.6.a, bf16[64,256]{1,0:T(8,128)(2,1)S(1)} %get-tuple-element.7.b, bf16[64,256]{1,0:T(8,128)(2,1)S(1)} %get-tuple-element.8.c), custom_call_target="tpu_custom_call" | custom-call | tf_op jit(solution)/shard_map/pallas_call | solution.py:538

commit v7 on v6

--- a/solution.py
+++ b/solution.py
@@ -132,10 +132,10 @@
     gb2 = [rows_to(CH + KB, place[NX - j] * 2 * CH + CH + KB, CH - KB, (gb2_s, gb2_r), j, xp(j)) for j in js]
     qx = [remote(qd.at[zh, part, core], qd.at[zh, part, core], qx_s.at[part], qx_r.at[part], mirror) for part in range(2)]
     qc = [remote(qd.at[1 - zh, part, core], qd.at[1 - zh, part, core], qc_s.at[part], qc_r.at[part], sibling) for part in range(2)]
+    qx[0].start()
+    qx[1].start()
     for copy in ga1 + gb1:
         copy.start()
-    qx[0].start()
-    qx[1].start()
     vx = remote(vis.at[zh], vis.at[zh], vx_s.at[0], vx_r.at[0], zp(NZL))
     vx.start()
     for copy in ga0 + gb0:

time: 51 us -> 51 us (level)
  no operation moved by 1% of the time
where the time goes in v7:
time: 51 us; the launch traced here: 50.8 us
  Pallas kernels  50 us (98%)
  between operations  0.8 us (2%)
    pallas_call x1, Pallas kernels, shards(): pl.pallas_call(kernel, out_shape=tuple((pltpu.VMEM(s, BF16) for s in shap...  49.4 us

profile of v7, /device:TPU:1, one launch (start us, length us, event | category | flops | bytes accessed | tf_op | source)
XLA Modules:
  0.0 50.8 jit_solution(936713318878904318)
XLA Ops:
  0.6 49.4 %shard_map.85 = (bf16[256,256]{1,0:T(8,128)(2,1)S(1)}, bf16[64,256]{1,0:T(8,128)(2,1)S(1)}, bf16[64,256]{1,0:T(8,128)(2,1)S(1)}) custom-call(bf16[256,256]{1,0:T(8,128)(2,1)} %q_in.1, bf16[256,256]{1,0:T(8,128)(2,1)} %g_in.1, bf16[64,256]{1,0:T(8,128)(2,1)} %k_in.1, bf16[64,256]{1,0:T(8,128)(2,1)} %v_in.1, s32[2,64]{1,0:T(2,128)} %vis_in.1, s32[1,64]{1,0:T(1,128)} %bitcast.1), custom_call_target="tpu_custom_call" | custom-call | tf_op jit(solution)/shard_map/pallas_call | solution.py:527
  50.0 0.7 %shard_map.86 = (bf16[256,256]{1,0:T(8,128)(2,1)}, bf16[64,256]{1,0:T(8,128)(2,1)}, bf16[64,256]{1,0:T(8,128)(2,1)}) custom-call(bf16[256,256]{1,0:T(8,128)(2,1)S(1)} %get-tuple-element.6.a, bf16[64,256]{1,0:T(8,128)(2,1)S(1)} %get-tuple-element.7.b, bf16[64,256]{1,0:T(8,128)(2,1)S(1)} %get-tuple-element.8.c), custom_call_target="tpu_custom_call" | custom-call | tf_op jit(solution)/shard_map/pallas_call | solution.py:538
